TPU v7x, 32 devices: a whole 2x2x4 slice. The times are simulated.
32 devices in a mesh: groups: 2 (over y), req: 16 (over z, x, core).
Axes of the slice: x: 2, y: 2, z: 4, core: 2. Of those that a mesh axis runs over, the one named last changes fastest.
Arguments:
- kv_cache: bfloat16 [1152, 2, 128, 512], P(('groups', 'req')), parts along dimension 0
- draft_rows: bfloat16 [1536, 5120], P(('groups', 'req')), parts along dimension 0
- cache_lengths: int32 [384], P('groups'), parts along dimension 0, may hold values from 1 to 384, as said below
- row_offsets: int32 [32], P('groups'), parts along dimension 0, may hold values from 0 to 15, as said below
- draft_order: int32 [1536], P(('groups', 'req')), parts along dimension 0, may hold values from 0 to 47, as said below
- pair_mask: int32 [2], P('groups'), parts along dimension 0, may hold values from 1 to 15
- moved_slots: int32 [32], P('groups'), parts along dimension 0, may hold values from 0 to 11
Outputs:
- verified: bfloat16 [1536, 4096], P(('groups', 'req')), parts along dimension 0
There are 2 independent parts, one for each index of `groups`. A program takes and returns all parts, laid end to end along the dimension named above; each array names one. Nothing has to cross between parts.
Inputs may be any that keep to these rules, and one draw needn't show every extreme that they name: `row_offsets`: all entries are different; the offsets 1, 15 and 8 are always among them. `draft_order`: each device's 48 entries are a permutation. `cache_lengths`: some request has exactly 384 positions.
All inputs are finite; a program needn't handle non-finite values.
Results may differ from a plain program's by a relative error of at most 0.0037.
Values may be sent and summed in bfloat16 or wider, within the bound.
A program may use at most 128 MiB of HBM per device.

v0:
```python
import jax
import jax.numpy as jnp
from jax import lax
from jax.sharding import PartitionSpec as P

QH = 32
KVH = 4
HD = 128
DRAFT = 4
PAGE = 128
R_DEV = 12
PPR = 3
QW = 4096
KVW = 512


def from_partner(value, axis, apart):
    return lax.ppermute(value, axis, [(i, i ^ 1 << apart) for i in range(lax.axis_size(axis))])


def attend_slots(page_pool, lengths, row_block):
    grp = QH // KVH
    slots = page_pool.shape[0]
    span = page_pool.shape[1] * page_pool.shape[3]
    cache_keys = page_pool[:, :, 0].reshape(slots, span, KVH, HD)
    cache_vals = page_pool[:, :, 1].reshape(slots, span, KVH, HD)
    queries = row_block[:, :, :QW].reshape(slots, DRAFT, KVH, grp, HD)
    new_keys = row_block[:, :, QW : QW + KVW].reshape(slots, DRAFT, KVH, HD)
    new_vals = row_block[:, :, QW + KVW :].reshape(slots, DRAFT, KVH, HD)
    factor = 1.0 / jnp.sqrt(jnp.float32(HD))
    cache_score = (
        jnp.einsum("rtghd,rlgd->rtghl", queries, cache_keys, preferred_element_type=jnp.float32)
        * factor
    )
    new_score = (
        jnp.einsum("rtghd,rugd->rtghu", queries, new_keys, preferred_element_type=jnp.float32)
        * factor
    )
    cache_valid = (jnp.arange(span, dtype=jnp.int32)[None, :] < lengths[:, None])[
        :, None, None, None, :
    ]
    positions = jnp.arange(DRAFT, dtype=jnp.int32)
    new_valid = (positions[None, :] <= positions[:, None])[None, :, None, None, :]
    cache_score = jnp.where(cache_valid, cache_score, jnp.float32(-1e30))
    new_score = jnp.where(new_valid, new_score, jnp.float32(-1e30))
    peak = jnp.maximum(jnp.max(cache_score, axis=-1), jnp.max(new_score, axis=-1))
    cache_weight = jnp.where(cache_valid, jnp.exp(cache_score - peak[..., None]), 0.0)
    new_weight = jnp.where(new_valid, jnp.exp(new_score - peak[..., None]), 0.0)
    denominator = jnp.sum(cache_weight, axis=-1) + jnp.sum(new_weight, axis=-1)
    summed = jnp.einsum(
        "rtghl,rlgd->rtghd",
        cache_weight.astype(jnp.bfloat16),
        cache_vals,
        preferred_element_type=jnp.float32,
    )
    summed = summed + jnp.einsum(
        "rtghu,rugd->rtghd",
        new_weight.astype(jnp.bfloat16),
        new_vals,
        preferred_element_type=jnp.float32,
    )
    return (summed / denominator[..., None]).reshape(slots, DRAFT, QW).astype(jnp.bfloat16)


def on_device(
    kv_cache, draft_rows, cache_lengths, row_offsets, draft_order, pair_mask, moved_slots
):
    count = lax.axis_size("req")
    own_index = lax.axis_index("req")
    sections = count.bit_length() - 1
    rows_here = draft_rows.shape[0]
    per_peer = max(1, rows_here // count)
    slot_total = count * per_peer
    place_ids = jnp.arange(slot_total, dtype=jnp.int32)
    targets = (own_index - row_offsets[draft_order // per_peer]) % count
    send_place = targets * per_peer + draft_order % per_peer
    send_map = (place_ids[:, None] == send_place[None, :]).astype(jnp.bfloat16)
    outgoing = jnp.dot(send_map, draft_rows, preferred_element_type=jnp.float32).astype(
        jnp.bfloat16
    )
    incoming = lax.all_to_all(outgoing, "req", split_axis=0, concat_axis=0, tiled=True)
    owner_rows = jnp.arange(rows_here, dtype=jnp.int32)
    sources = (own_index + row_offsets[owner_rows // per_peer]) % count
    recv_place = sources * per_peer + owner_rows % per_peer
    recv_map = (recv_place[:, None] == place_ids[None, :]).astype(jnp.bfloat16)
    owned = jnp.dot(recv_map, incoming, preferred_element_type=jnp.float32).astype(jnp.bfloat16)
    owned = owned.reshape(R_DEV, DRAFT, owned.shape[-1])
    my_slot = moved_slots[own_index]
    page_pool = kv_cache.reshape(R_DEV, PPR, 2, PAGE, kv_cache.shape[-1])
    visitor = lax.dynamic_index_in_dim(owned, my_slot, 0, keepdims=False)
    for section in range(sections):
        arrived = from_partner(visitor, "req", section)
        visitor = jnp.where(
            jnp.bitwise_and(jnp.right_shift(pair_mask[0], section), 1) == 1, arrived, visitor
        )
    queries = lax.dynamic_update_index_in_dim(owned, visitor, my_slot, 0)
    lengths = lax.dynamic_slice_in_dim(cache_lengths, own_index * R_DEV, R_DEV)
    results = attend_slots(page_pool, lengths, queries)
    answer = lax.dynamic_index_in_dim(results, my_slot, 0, keepdims=False)
    for section in range(sections):
        arrived = from_partner(answer, "req", section)
        answer = jnp.where(
            jnp.bitwise_and(jnp.right_shift(pair_mask[0], section), 1) == 1, arrived, answer
        )
    results = lax.dynamic_update_index_in_dim(results, answer, my_slot, 0)
    flat_results = results.reshape(R_DEV * DRAFT, results.shape[-1])
    backward = jnp.dot(recv_map.T, flat_results, preferred_element_type=jnp.float32).astype(
        jnp.bfloat16
    )
    returned = lax.all_to_all(backward, "req", split_axis=0, concat_axis=0, tiled=True)
    return jnp.dot(send_map.T, returned, preferred_element_type=jnp.float32).astype(jnp.bfloat16)


def solution(mesh):
    in_specs = (
        P(("groups", "req"), None, None, None),
        P(("groups", "req"), None),
        P("groups"),
        P("groups"),
        P(("groups", "req")),
        P("groups"),
        P("groups"),
    )
    out_specs = P(("groups", "req"), None)
    return jax.shard_map(
        on_device, mesh=mesh, in_specs=in_specs, out_specs=out_specs, check_vma=False
    )
```

profile of v0, /device:TPU:0, one launch (start us, length us, event | category | flops | bytes accessed | tf_op | source)
XLA Modules:
  0.0 107.0 jit_solution(16687061333840150898)
XLA Ops:
  0.0 0.7 compare_select_fusion.1
  0.7 1.4 %gather_fusion = s32[48]{0:T(128)S(1)} fusion(s32[16]{0:T(128)} %param.10, s32[1024]{0:T(1024)S(1)} %pad_clamp_fusion.1), kind=kCustom, calls=%fused_computation | custom fusion | bytes 576 | tf_op jit(solution)/shard_map/gather | solution.py:75
  2.2 0.7 fusion.35
  3.1 1.1 %all_to_all.16 = bf16[16,3,5120]{2,1,0:T(4,128)(2,1)} reshape(bf16[48,5120]{1,0:T(8,128)(2,1)S(1)} %convolution_convert_fusion.1) | data formatting | bytes 983040 | tf_op jit(solution)/shard_map/all_to_all | solution.py:81
  4.3 7.4 %all-to-all-start = ((bf16[16,3,5120]{2,1,0:T(4,128)(2,1)}), bf16[16,3,5120]{2,1,0:T(4,128)(2,1)S(1)}, u32[]{:S(2)}, u32[]{:S(2)}) async-start(bf16[16,3,5120]{2,1,0:T(4,128)(2,1)} %all_to_all.16), calls=%async_computation | async-start | bytes 1310720 | tf_op jit(solution)/shard_map/all_to_all | solution.py:81
  11.7 0.8 gather_fusion.1
  12.5 0.6 dynamic_slice.15
  15.0 13.2 %all-to-all-done = bf16[16,3,5120]{2,1,0:T(4,128)(2,1)S(1)} async-done(((bf16[16,3,5120]{2,1,0:T(4,128)(2,1)}), bf16[16,3,5120]{2,1,0:T(4,128)(2,1)S(1)}, u32[]{:S(2)}, u32[]{:S(2)}) %all-to-all-start) | async-done | bytes 491552 | tf_op jit(solution)/shard_map/all_to_all | solution.py:81
  30.0 0.5 collective-permute-done
  30.5 1.2 %collective-permute-start.1 = (bf16[4,5120]{1,0:T(4,128)(2,1)S(1)}, bf16[4,5120]{1,0:T(4,128)(2,1)S(1)}, u32[]{:S(2)}, u32[]{:S(2)}) collective-permute-start(bf16[4,5120]{1,0:T(4,128)(2,1)S(1)} %broadcast_select_fusion), channel_id=1, source_target_pairs={{0,2},{1,3},{2,0},{3,1},{4,6},{5,7},{6,4},{7,5},{8,10},{9,11},{10,... | collective-permute-start | bytes 122888 | tf_op jit(solution)/shard_map/ppermute | solution.py:18
  31.8 8.6 %slice_bitcast_fusion.1 = (bf16[12,3,1,128,512]{4,3,1,0,2:T(8,128)(2,1)}, bf16[12,3,1,128,512]{4,3,1,0,2:T(8,128)(2,1)}) fusion(bf16[12,3,2,128,512]{4,3,2,1,0:T(8,128)(2,1)} %bitcast.83), kind=kLoop, calls=%fused_computation.5 | loop fusion | bytes 18874368
  40.5 2.0 %collective-permute-start.2 = (bf16[4,5120]{1,0:T(4,128)(2,1)S(1)}, bf16[4,5120]{1,0:T(4,128)(2,1)S(1)}, u32[]{:S(2)}, u32[]{:S(2)}) collective-permute-start(bf16[4,5120]{1,0:T(4,128)(2,1)S(1)} %broadcast_select_fusion.1), channel_id=1, source_target_pairs={{0,4},{1,5},{2,6},{3,7},{4,0},{5,1},{6,2},{7,3},{8,12},{9,13},{10,... | collective-permute-start | bytes 122888 | tf_op jit(solution)/shard_map/ppermute | solution.py:18
  42.5 2.0 %collective-permute-done.2 = bf16[4,5120]{1,0:T(4,128)(2,1)S(1)} collective-permute-done((bf16[4,5120]{1,0:T(4,128)(2,1)S(1)}, bf16[4,5120]{1,0:T(4,128)(2,1)S(1)}, u32[]{:S(2)}, u32[]{:S(2)}) %collective-permute-start.2) | collective-permute-done | bytes 40992 | tf_op jit(solution)/shard_map/ppermute | solution.py:18
  44.6 1.8 %collective-permute-start.3 = (bf16[4,5120]{1,0:T(4,128)(2,1)S(1)}, bf16[4,5120]{1,0:T(4,128)(2,1)S(1)}, u32[]{:S(2)}, u32[]{:S(2)}) collective-permute-start(bf16[4,5120]{1,0:T(4,128)(2,1)S(1)} %broadcast_select_fusion.2), channel_id=1, source_target_pairs={{0,8},{1,9},{2,10},{3,11},{4,12},{5,13},{6,14},{7,15},{8,0},{9,1},... | collective-permute-start | bytes 122888 | tf_op jit(solution)/shard_map/ppermute | solution.py:18
  46.4 7.7 %reshape_squeeze.7 = bf16[12,384,4,128]{3,2,1,0:T(4,128)(2,1)} reshape(bf16[12,3,1,128,512]{4,3,1,0,2:T(8,128)(2,1)} %get-tuple-element.6) | data formatting | bytes 9437184 | tf_op jit(solution)/shard_map/reshape;squeeze | solution.py:26
  54.1 7.7 %reshape_squeeze.6 = bf16[12,384,4,128]{3,2,1,0:T(4,128)(2,1)} reshape(bf16[12,3,1,128,512]{4,3,1,0,2:T(8,128)(2,1)} %get-tuple-element.5) | data formatting | bytes 9437184 | tf_op jit(solution)/shard_map/reshape;squeeze | solution.py:25
  62.1 0.4 reshape.154
  62.5 1.9 %fusion.46 = (f32[12,4,4,8]{3,1,2,0:T(4,128)S(1)}, f32[12,4,4,8,4]{3,4,1,2,0:T(4,128)S(1)}) fusion(bf16[12,4,4,8,128]{4,3,2,1,0:T(8,128)(2,1)S(1)} %reshape.154, bf16[12,4,5120]{2,1,0:T(4,128)(2,1)S(1)} %bitcast_dynamic-update-slice_fusion, pred[4,4]{1,0:T(4,128)(4,1)S(1)} %iota_compare_fusion.7), kind=kOutput, calls=%fused_computation.89 | convolution fusion | flops 1589760 | bytes 473600 | tf_op jit(solution)/shard_map/rtghd,rugd->rtghu/dot_general | solution.py:36
  64.4 4.3 %bitcast_reduce_fusion = (f32[12,4,4,8]{3,1,2,0:T(4,128)S(1)}, f32[12,4,4,8,384]{4,3,2,1,0:T(8,128)S(1)}) fusion(pred[12,384]{1,0:T(8,128)(4,1)S(1)} %iota_compare_fusion, bf16[12,384,4,128,1]{3,2,1,0,4:T(4,128)(2,1)} %bitcast.82, bf16[12,4,4,8,128]{4,3,2,1,0:T(8,128)(2,1)S(1)} %reshape.154), kind=kOutput, calls=%fused_computation.13 | convolution fusion | flops 152762880 | bytes 7481856 | tf_op jit(solution)/shard_map/rtghd,rlgd->rtghl/dot_general | solution.py:32
  68.8 0.9 fusion.6
  69.7 1.2 %fusion.8 = f32[12,4,4,8,128]{4,3,1,2,0:T(8,128)S(1)} fusion(bf16[12,384,4,128,1]{3,2,1,0,4:T(4,128)(2,1)S(1)} %bitcast.86, f32[12,4,4,8,384]{4,3,2,1,0:T(8,128)S(1)} %get-tuple-element.8, f32[12,4,4,8]{3,1,2,0:T(4,128)S(1)} %max.7, pred[12,384]{1,0:T(8,128)(4,1)S(1)} %iota_compare_fusion), kind=kOutput, calls=%fused_computation.19 | convolution fusion | flops 153944064 | bytes 7875072 | tf_op jit(solution)/shard_map/rtghl,rlgd->rtghd/dot_general | solution.py:50
  70.9 0.4 fusion.25
  71.4 0.5 fusion.13
  72.2 1.2 %collective-permute-done.4 = bf16[4,4096]{1,0:T(4,128)(2,1)S(1)} collective-permute-done((bf16[4,4096]{1,0:T(4,128)(2,1)S(1)}, bf16[4,4096]{1,0:T(4,128)(2,1)S(1)}, u32[]{:S(2)}, u32[]{:S(2)}) %collective-permute-start.4) | collective-permute-done | bytes 32800 | tf_op jit(solution)/shard_map/ppermute | solution.py:18
  73.4 2.1 %collective-permute-start.5 = (bf16[4,4096]{1,0:T(4,128)(2,1)S(1)}, bf16[4,4096]{1,0:T(4,128)(2,1)S(1)}, u32[]{:S(2)}, u32[]{:S(2)}) collective-permute-start(bf16[4,4096]{1,0:T(4,128)(2,1)S(1)} %broadcast_select_fusion.3), channel_id=1, source_target_pairs={{0,2},{1,3},{2,0},{3,1},{4,6},{5,7},{6,4},{7,5},{8,10},{9,11},{10,... | collective-permute-start | bytes 98312 | tf_op jit(solution)/shard_map/ppermute | solution.py:18
  75.5 1.9 %collective-permute-done.5 = bf16[4,4096]{1,0:T(4,128)(2,1)S(1)} collective-permute-done((bf16[4,4096]{1,0:T(4,128)(2,1)S(1)}, bf16[4,4096]{1,0:T(4,128)(2,1)S(1)}, u32[]{:S(2)}, u32[]{:S(2)}) %collective-permute-start.5) | collective-permute-done | bytes 32800 | tf_op jit(solution)/shard_map/ppermute | solution.py:18
  77.4 1.6 %collective-permute-start.6 = (bf16[4,4096]{1,0:T(4,128)(2,1)S(1)}, bf16[4,4096]{1,0:T(4,128)(2,1)S(1)}, u32[]{:S(2)}, u32[]{:S(2)}) collective-permute-start(bf16[4,4096]{1,0:T(4,128)(2,1)S(1)} %broadcast_select_fusion.4), channel_id=1, source_target_pairs={{0,4},{1,5},{2,6},{3,7},{4,0},{5,1},{6,2},{7,3},{8,12},{9,13},{10,... | collective-permute-start | bytes 98312 | tf_op jit(solution)/shard_map/ppermute | solution.py:18
  79.0 2.3 %collective-permute-done.6 = bf16[4,4096]{1,0:T(4,128)(2,1)S(1)} collective-permute-done((bf16[4,4096]{1,0:T(4,128)(2,1)S(1)}, bf16[4,4096]{1,0:T(4,128)(2,1)S(1)}, u32[]{:S(2)}, u32[]{:S(2)}) %collective-permute-start.6) | collective-permute-done | bytes 32800 | tf_op jit(solution)/shard_map/ppermute | solution.py:18
  81.4 1.2 %collective-permute-start.7 = (bf16[4,4096]{1,0:T(4,128)(2,1)S(1)}, bf16[4,4096]{1,0:T(4,128)(2,1)S(1)}, u32[]{:S(2)}, u32[]{:S(2)}) collective-permute-start(bf16[4,4096]{1,0:T(4,128)(2,1)S(1)} %broadcast_select_fusion.5), channel_id=1, source_target_pairs={{0,8},{1,9},{2,10},{3,11},{4,12},{5,13},{6,14},{7,15},{8,0},{9,1},... | collective-permute-start | bytes 98312 | tf_op jit(solution)/shard_map/ppermute | solution.py:18
  82.6 3.7 %collective-permute-done.7 = bf16[4,4096]{1,0:T(4,128)(2,1)S(1)} collective-permute-done((bf16[4,4096]{1,0:T(4,128)(2,1)S(1)}, bf16[4,4096]{1,0:T(4,128)(2,1)S(1)}, u32[]{:S(2)}, u32[]{:S(2)}) %collective-permute-start.7) | collective-permute-done | bytes 32800 | tf_op jit(solution)/shard_map/ppermute | solution.py:18
  87.0 18.5 %all_to_all.24 = bf16[16,3,4096]{2,1,0:T(4,128)(2,1)S(1)} all-to-all(bf16[16,3,4096]{2,1,0:T(4,128)(2,1)S(1)} %all_to_all.19), channel_id=1, replica_groups=mesh['groups'=2,'req'=16] {'req'}, dimensions={0} | all-to-all | bytes 786432 | tf_op jit(solution)/shard_map/all_to_all | solution.py:110
  105.9 1.1 convolution_convert_fusion.2
  (47 shorter events, 3.3 us)
Async XLA Ops:
  0.0 2.9 %copy-start = (bf16[48,5120]{1,0:T(8,128)(2,1)S(1)}, bf16[48,5120]{1,0:T(8,128)(2,1)}, u32[]{:S(2)}) copy-start(bf16[48,5120]{1,0:T(8,128)(2,1)} %param.8) | copy-start | bytes 1474564
  0.0 11.7 %copy-start.1 = (s32[16]{0:T(128)S(1)}, s32[16]{0:T(128)}, u32[]{:S(2)}) copy-start(s32[16]{0:T(128)} %param.10) | copy-start | bytes 196
  0.0 12.4 %copy-start.3 = (s32[16]{0:T(128)S(1)}, s32[16]{0:T(128)}, u32[]{:S(2)}) copy-start(s32[16]{0:T(128)} %param.13) | copy-start | bytes 196
  4.3 24.0 %all-to-all-start = ((bf16[16,3,5120]{2,1,0:T(4,128)(2,1)}), bf16[16,3,5120]{2,1,0:T(4,128)(2,1)S(1)}, u32[]{:S(2)}, u32[]{:S(2)}) async-start(bf16[16,3,5120]{2,1,0:T(4,128)(2,1)} %all_to_all.16), calls=%async_computation | async-start | bytes 1310720 | tf_op jit(solution)/shard_map/all_to_all | solution.py:81
  29.2 1.3 %collective-permute-start = (bf16[4,5120]{1,0:T(4,128)(2,1)S(1)}, bf16[4,5120]{1,0:T(4,128)(2,1)S(1)}, u32[]{:S(2)}, u32[]{:S(2)}) collective-permute-start(bf16[4,5120]{1,0:T(4,128)(2,1)S(1)} %dynamic-slice_bitcast_fusion), channel_id=1, source_target_pairs={{0,1},{1,0},{2,3},{3,2},{4,5},{5,4},{6,7},{7,6},{8,9},{9,8},{10,11... | collective-permute-start | bytes 122888 | tf_op jit(solution)/shard_map/ppermute | solution.py:18
  30.5 9.9 %collective-permute-start.1 = (bf16[4,5120]{1,0:T(4,128)(2,1)S(1)}, bf16[4,5120]{1,0:T(4,128)(2,1)S(1)}, u32[]{:S(2)}, u32[]{:S(2)}) collective-permute-start(bf16[4,5120]{1,0:T(4,128)(2,1)S(1)} %broadcast_select_fusion), channel_id=1, source_target_pairs={{0,2},{1,3},{2,0},{3,1},{4,6},{5,7},{6,4},{7,5},{8,10},{9,11},{10,... | collective-permute-start | bytes 122888 | tf_op jit(solution)/shard_map/ppermute | solution.py:18
  31.8 8.6 %copy-start.2 = (s32[192]{0:T(256)S(1)}, s32[192]{0:T(256)}, u32[]{:S(2)}) copy-start(s32[192]{0:T(256)} %param.9) | copy-start | bytes 2308
  40.5 4.1 %collective-permute-start.2 = (bf16[4,5120]{1,0:T(4,128)(2,1)S(1)}, bf16[4,5120]{1,0:T(4,128)(2,1)S(1)}, u32[]{:S(2)}, u32[]{:S(2)}) collective-permute-start(bf16[4,5120]{1,0:T(4,128)(2,1)S(1)} %broadcast_select_fusion.1), channel_id=1, source_target_pairs={{0,4},{1,5},{2,6},{3,7},{4,0},{5,1},{6,2},{7,3},{8,12},{9,13},{10,... | collective-permute-start | bytes 122888 | tf_op jit(solution)/shard_map/ppermute | solution.py:18
  44.6 17.3 %collective-permute-start.3 = (bf16[4,5120]{1,0:T(4,128)(2,1)S(1)}, bf16[4,5120]{1,0:T(4,128)(2,1)S(1)}, u32[]{:S(2)}, u32[]{:S(2)}) collective-permute-start(bf16[4,5120]{1,0:T(4,128)(2,1)S(1)} %broadcast_select_fusion.2), channel_id=1, source_target_pairs={{0,8},{1,9},{2,10},{3,11},{4,12},{5,13},{6,14},{7,15},{8,0},{9,1},... | collective-permute-start | bytes 122888 | tf_op jit(solution)/shard_map/ppermute | solution.py:18
  64.3 5.3 %slice-start = ((s8[4718592]{0:T(1024)(128)(4,1)}), s8[4194304]{0:T(1024)(128)(4,1)S(1)}, s32[]{:S(2)}) async-start(s8[4718592]{0:T(1024)(128)(4,1)} %bitcast.84), calls=%async_computation.2 | async-start | bytes 8388608
  64.4 5.3 %slice-start.1 = ((s8[4718592]{0:T(1024)(128)(4,1)}), s8[524288]{0:T(1024)(128)(4,1)S(1)}, s32[]{:S(2)}) async-start(s8[4718592]{0:T(1024)(128)(4,1)} %bitcast.84), calls=%async_computation.3 | async-start | bytes 1048576
  72.1 1.3 %collective-permute-start.4 = (bf16[4,4096]{1,0:T(4,128)(2,1)S(1)}, bf16[4,4096]{1,0:T(4,128)(2,1)S(1)}, u32[]{:S(2)}, u32[]{:S(2)}) collective-permute-start(bf16[4,4096]{1,0:T(4,128)(2,1)S(1)} %dynamic-slice_bitcast_fusion.1), channel_id=1, source_target_pairs={{0,1},{1,0},{2,3},{3,2},{4,5},{5,4},{6,7},{7,6},{8,9},{9,8},{10,11... | collective-permute-start | bytes 98312 | tf_op jit(solution)/shard_map/ppermute | solution.py:18
  73.4 4.0 %collective-permute-start.5 = (bf16[4,4096]{1,0:T(4,128)(2,1)S(1)}, bf16[4,4096]{1,0:T(4,128)(2,1)S(1)}, u32[]{:S(2)}, u32[]{:S(2)}) collective-permute-start(bf16[4,4096]{1,0:T(4,128)(2,1)S(1)} %broadcast_select_fusion.3), channel_id=1, source_target_pairs={{0,2},{1,3},{2,0},{3,1},{4,6},{5,7},{6,4},{7,5},{8,10},{9,11},{10,... | collective-permute-start | bytes 98312 | tf_op jit(solution)/shard_map/ppermute | solution.py:18
  77.4 4.0 %collective-permute-start.6 = (bf16[4,4096]{1,0:T(4,128)(2,1)S(1)}, bf16[4,4096]{1,0:T(4,128)(2,1)S(1)}, u32[]{:S(2)}, u32[]{:S(2)}) collective-permute-start(bf16[4,4096]{1,0:T(4,128)(2,1)S(1)} %broadcast_select_fusion.4), channel_id=1, source_target_pairs={{0,4},{1,5},{2,6},{3,7},{4,0},{5,1},{6,2},{7,3},{8,12},{9,13},{10,... | collective-permute-start | bytes 98312 | tf_op jit(solution)/shard_map/ppermute | solution.py:18
  81.4 4.9 %collective-permute-start.7 = (bf16[4,4096]{1,0:T(4,128)(2,1)S(1)}, bf16[4,4096]{1,0:T(4,128)(2,1)S(1)}, u32[]{:S(2)}, u32[]{:S(2)}) collective-permute-start(bf16[4,4096]{1,0:T(4,128)(2,1)S(1)} %broadcast_select_fusion.5), channel_id=1, source_target_pairs={{0,8},{1,9},{2,10},{3,11},{4,12},{5,13},{6,14},{7,15},{8,0},{9,1},... | collective-permute-start | bytes 98312 | tf_op jit(solution)/shard_map/ppermute | solution.py:18
where the time goes:
time: 108 us; the launch traced here: 107 us
  local copies, waits for them, and re-layouts  30.1 us (28%)
  waiting for transfers between devices  24.9 us (23%)
  blocking collectives  18.5 us (17%)
  starting transfers between devices  17.5 us (16%)
  matrix products  9.96 us (9%)
  other arithmetic  3.14 us (3%)
  between operations  2.85 us (3%)
    all_to_all x1, blocking collectives, on_device(): lax.all_to_all(backward, 'req', split_axis=0, concat_axis=0, tiled=True)  18.5 us
    all_to_all x1, waiting for transfers between devices, on_device(): lax.all_to_all(outgoing, 'req', split_axis=0, concat_axis=0, tiled=True)  13.2 us
    ppermute x8, waiting for transfers between devices, from_partner(): lax.ppermute(value, axis, [(i, i ^ 1 << apart) for i in range(lax.axis_si...  11.6 us
    ppermute x8, starting transfers between devices, from_partner(): lax.ppermute(value, axis, [(i, i ^ 1 << apart) for i in range(lax.axis_si...  10.2 us
    unnamed x13, local copies, waits for them, and re-layouts  8.61 us
    another operation x1, local copies, waits for them, and re-layouts, attend_slots(): cache_vals = page_pool[:, :, 1].reshape(slots, span, KVH, HD)  7.73 us
    another operation x1, local copies, waits for them, and re-layouts, attend_slots(): cache_keys = page_pool[:, :, 0].reshape(slots, span, KVH, HD)  7.7 us
    all_to_all x1, starting transfers between devices, on_device(): lax.all_to_all(outgoing, 'req', split_axis=0, concat_axis=0, tiled=True)  7.37 us
  transfers between devices with their start and end apart: 9, of which 7 were waited for; matrix products, arithmetic and copies ran while one was open for 24% of the time, Pallas kernels for 0%

commit v1 on v0

v1 whole, which is shorter than its diff:
```python
import functools

import jax
import jax.numpy as jnp
from jax import lax
from jax.experimental import pallas as pl
from jax.experimental.pallas import tpu as pltpu
from jax.sharding import PartitionSpec as P

HD = 128
DRAFT = 4
PAGE = 128
R_DEV = 12
PPR = 3
QW = 4096
KVW = 512
GRP = 8
CHUNKS = 2
HEADS = QW // HD // CHUNKS
KV_HERE = KVW // HD // CHUNKS
PARTS = 5
PART_W = (QW + 2 * KVW) // CHUNKS // PARTS
Q_PARTS = HEADS * HD // PART_W
PART_HEADS = PART_W // HD
F32 = jnp.float32
BF16 = jnp.bfloat16
MESH = pl.DeviceIdType.MESH


def iota(shape, dim):
    return lax.broadcasted_iota(jnp.int32, shape, dim)


def small_div(x, c):
    return x if c == 1 else lax.shift_right_logical(x * (65536 // c + 1), 16)


def small_mod(x, c):
    return x - small_div(x, c) * c


def wrap(x, n):
    x = jnp.where(x < 0, x + n, x)
    return jnp.where(x >= n, x - n, x)


def lane_sum(hit, value):
    return jnp.sum(jnp.where(hit, value, 0).astype(F32), axis=1, keepdims=True).astype(jnp.int32)


def row_sum(hit, value):
    return jnp.sum(jnp.where(hit, value, 0).astype(F32), axis=0, keepdims=True).astype(jnp.int32)


def pick(columns, width):
    return (iota((columns.shape[0], width), 1) == columns).astype(F32).astype(BF16)


def dot(a, b):
    return jnp.dot(a, b, preferred_element_type=F32)


def dot_t(a, b):
    return lax.dot_general(a, b, (((1,), (1,)), ((), ())), preferred_element_type=F32)


def flip(device, delta):
    bit = 0
    out = device
    while delta >> bit:
        if (delta >> bit) & 1:
            out = out + (1 << bit) * (1 - 2 * ((device // (1 << bit)) % 2))
        bit += 1
    return out


def digits_of(n):
    bits = n.bit_length() - 1
    return [(b, 1 << min(2, bits - b)) for b in range(0, bits, 2)]


def kernel(
    n, cap, lengths, mask, moved, order_ref, off_ref, draft_ref, kv_hbm, out_ref,
    kv, send, recv, rows, res, back, home, xs, xr, ys, yr,
    kv_sem, send_sem, recv_sem, back_sem, home_sem, xs_sem, xr_sem, ys_sem, yr_sem,
):
    me = lax.axis_index("req")
    n_rows = order_ref.shape[1]
    block = send.shape[2]
    n_off = off_ref.shape[1]
    digits = digits_of(n)

    kv_copy = pltpu.make_async_copy(kv_hbm, kv, kv_sem)
    kv_copy.start()

    def peer_of(i):
        step = (i + n // 2 - 1) % (n - 1) + 1
        return (me + step) % n

    barrier = pltpu.get_barrier_semaphore()

    def greet(i, carry):
        pl.semaphore_signal(barrier, inc=1, device_id={"req": peer_of(i)}, device_id_type=MESH)
        return carry

    lax.fori_loop(0, n - 1, greet, 0)

    order = order_ref[...]
    off = off_ref[...]
    order_col = lane_sum(iota((n_rows, n_rows), 0) == iota((n_rows, n_rows), 1), order)
    off_of_row = lane_sum(iota((n_rows, n_off), 1) == small_div(order_col, cap), off)
    owner = wrap(me - off_of_row, n)
    place = small_mod(order_col, cap)
    wide = PARTS * n_rows
    col = iota((1, wide), 1)
    target = owner * block + place
    target = row_sum(iota((n_rows, wide), 0) == small_mod(col, n_rows), target)
    target = target + small_div(col, n_rows) * cap
    pack = (iota((n * block, wide), 0) == target).astype(F32).astype(BF16)

    def exchange(shape_send, shape_recv, s_sem, r_sem, c, peer):
        return pltpu.make_async_remote_copy(
            src_ref=shape_send.at[c, peer], dst_ref=shape_recv.at[c, me],
            send_sem=s_sem.at[c, peer], recv_sem=r_sem.at[c, me],
            device_id={"req": peer}, device_id_type=MESH,
        )

    def send_all(s_ref, r_ref, s_sem, r_sem, c):
        def body(i, carry):
            exchange(s_ref, r_ref, s_sem, r_sem, c, peer_of(i)).start()
            return carry

        lax.fori_loop(0, n - 1, body, 0)
        r_ref[c, me] = s_ref[c, me]

    def wait_recv(s_ref, r_ref, s_sem, r_sem, c):
        def body(i, carry):
            src = peer_of(i)
            pltpu.make_async_remote_copy(
                src_ref=s_ref.at[c, src], dst_ref=r_ref.at[c, src],
                send_sem=s_sem.at[c, src], recv_sem=r_sem.at[c, src],
                device_id={"req": src}, device_id_type=MESH,
            ).wait_recv()
            return carry

        lax.fori_loop(0, n - 1, body, 0)

    def wait_send(s_ref, r_ref, s_sem, r_sem, c):
        def body(i, carry):
            exchange(s_ref, r_ref, s_sem, r_sem, c, peer_of(i)).wait_send()
            return carry

        lax.fori_loop(0, n - 1, body, 0)

    for c in range(CHUNKS):
        q0 = c * HEADS * HD
        kw = KV_HERE * HD
        keys = draft_ref[:, QW + c * kw : QW + (c + 1) * kw]
        vals = draft_ref[:, QW + KVW + c * kw : QW + KVW + (c + 1) * kw]
        parts = [draft_ref[:, q0 + p * PART_W : q0 + (p + 1) * PART_W] for p in range(Q_PARTS)]
        stacked = jnp.concatenate(parts + [jnp.concatenate([keys, vals], axis=1)], axis=0)
        send[c] = dot(pack, stacked).astype(BF16).reshape(n, block, PART_W)
        if c == 0:
            pl.semaphore_wait(barrier, n - 1)
        send_all(send, recv, send_sem, recv_sem, c)

    my_slot = moved[me]
    pair = mask[0]
    r_col = iota((wide, 1), 0)
    k_col = small_mod(r_col, n_rows)
    off_col = lane_sum(iota((wide, n_off), 1) == small_div(k_col, cap), off)
    source = wrap(me + off_col, n)
    from_col = source * block + small_div(r_col, n_rows) * cap + small_mod(k_col, cap)
    is_moved = lax.shift_right_logical(k_col, 2) == my_slot
    unpack = pick(jnp.where(is_moved, -1, from_col), n * block)
    x_row = iota((4 * DRAFT, 1), 0)
    x_draft = small_mod(x_row, DRAFT)
    x_k = my_slot * DRAFT + x_draft
    x_off = lane_sum(iota((4 * DRAFT, n_off), 1) == small_div(x_k, cap), off)
    x_from = wrap(me + x_off, n) * block + small_mod(x_k, cap)
    x_tile = small_div(x_row, DRAFT)
    x_pick = pick(x_from + x_tile * cap, n * block)
    x_last = [pick(jnp.where(x_tile == i, x_from + Q_PARTS * cap, -1), n * block) for i in range(4)]
    q_rows = Q_PARTS * n_rows
    x_in = pick(
        jnp.where(is_moved, small_div(r_col, n_rows) * DRAFT + small_mod(k_col, DRAFT), -1)[:q_rows],
        4 * DRAFT,
    )
    last_moved = is_moved[q_rows:]
    last_draft = small_mod(k_col, DRAFT)[q_rows:]
    x_in_last = [pick(jnp.where(last_moved, i * DRAFT + last_draft, -1), 4 * DRAFT) for i in range(4)]
    flat = HEADS * n_rows
    y_row = iota((HEADS * DRAFT, 1), 0)
    y_pick = pick(
        small_div(y_row, DRAFT) * n_rows + my_slot * DRAFT + small_mod(y_row, DRAFT), flat
    )
    f_row = iota((flat, 1), 0)
    f_k = small_mod(f_row, n_rows)
    f_head = small_div(f_row, n_rows)
    f_moved = lax.shift_right_logical(f_k, 2) == my_slot
    y_in = pick(f_head * DRAFT + small_mod(f_k, DRAFT), HEADS * DRAFT)
    p_row = iota((n * HEADS, 1), 0)
    p_peer = small_div(p_row, HEADS)
    p_hit = p_peer == wrap(me + off, n)
    p_index = lane_sum(p_hit, iota((1, n_off), 1) + 1) - 1
    p_base = small_mod(p_row, HEADS) * n_rows + p_index * cap

    def swap(cur, s_ref, r_ref, s_sem, r_sem, c):
        slot = 0
        for shift, values in digits:
            s_ref[c, slot] = cur
            copies = []
            for delta in range(1, values):
                copies.append(
                    pltpu.make_async_remote_copy(
                        src_ref=s_ref.at[c, slot], dst_ref=r_ref.at[c, slot + delta - 1],
                        send_sem=s_sem.at[c, slot + delta - 1],
                        recv_sem=r_sem.at[c, slot + delta - 1],
                        device_id={"req": flip(me, delta << shift)}, device_id_type=MESH,
                    )
                )
                copies[-1].start()
            yield
            digit = jnp.bitwise_and(jnp.right_shift(pair, shift), values - 1)
            for delta in range(1, values):
                copies[delta - 1].wait()
                cur = jnp.where(digit == delta, r_ref[c, slot + delta - 1], cur)
            slot += values - 1
        return cur

    half = DRAFT
    rows_p = 2 * DRAFT
    span = PPR * PAGE
    factor = 1.0 / jnp.sqrt(F32(HD))
    block_row = small_mod(iota((GRP * rows_p, 1), 0), rows_p)
    first = block_row < half
    n_col = iota((GRP * rows_p, rows_p), 1)
    new_ok = (lax.shift_right_logical(n_col, 2) == lax.shift_right_logical(block_row, 2)) & (
        n_col <= block_row
    )
    position = iota((GRP * rows_p, span), 1)

    def attend(c):
        def body(pr, carry):
            at = pl.multiple_of(pr * rows_p, rows_p)
            slot = pr * 2
            limit = jnp.where(first, lengths[me * R_DEV + slot], lengths[me * R_DEV + slot + 1])
            ok = position < limit

            def cached(which, g):
                lanes = slice((c * KV_HERE + g) * HD, (c * KV_HERE + g + 1) * HD)
                return jnp.concatenate(
                    [kv[pl.ds((slot + a) * PPR, PPR), which, :, lanes].reshape(span, HD) for a in (0, 1)],
                    axis=1,
                )

            for g in range(KV_HERE):
                tiles = []
                for h in range(GRP):
                    p, i = divmod(g * GRP + h, PART_HEADS)
                    tiles.append(rows[c, pl.ds(p * n_rows + at, rows_p), i * HD : (i + 1) * HD])
                q = jnp.concatenate(tiles, axis=0)
                last = pl.ds(Q_PARTS * n_rows + at, rows_p)
                new_k = rows[c, last, g * HD : (g + 1) * HD].astype(BF16)
                new_v = rows[c, last, (KV_HERE + g) * HD : (KV_HERE + g + 1) * HD].astype(BF16)
                q2 = jnp.concatenate([jnp.where(first, q, 0.0), jnp.where(first, 0.0, q)], axis=1)
                score = dot_t(q2.astype(BF16), cached(0, g)) * factor
                new_score = dot_t(q.astype(BF16), new_k) * factor
                score = jnp.where(ok, score, -1e30)
                new_score = jnp.where(new_ok, new_score, -1e30)
                peak = jnp.maximum(
                    jnp.max(score, axis=1, keepdims=True), jnp.max(new_score, axis=1, keepdims=True)
                )
                w = jnp.where(ok, jnp.exp(score - peak), 0.0)
                new_w = jnp.where(new_ok, jnp.exp(new_score - peak), 0.0)
                total = jnp.sum(w, axis=1, keepdims=True) + jnp.sum(new_w, axis=1, keepdims=True)
                both = dot(w.astype(BF16), cached(1, g))
                out = jnp.where(first, both[:, :HD], both[:, HD:]) + dot(new_w.astype(BF16), new_v)
                out = (out / total).reshape(GRP, rows_p, HD)
                res[c, g * GRP : (g + 1) * GRP, pl.ds(at, rows_p), :] = out
            return carry

        lax.fori_loop(0, R_DEV // 2, body, 0)

    def work(c):
        wait_recv(send, recv, send_sem, recv_sem, c)
        got = recv[c].reshape(n * block, PART_W)
        last = sum(dot(x_last[i], got[:, i * HD : (i + 1) * HD]) for i in range(4))
        mine = jnp.concatenate([dot(x_pick, got), last], axis=1).astype(BF16)
        own = dot(unpack, got)
        visitor = yield from swap(mine, xs, xr, xs_sem, xr_sem, c)
        tail = visitor[:, PART_W:]
        added = jnp.concatenate(
            [dot(x_in, visitor[:, :PART_W]),
             jnp.concatenate([dot(m, tail) for m in x_in_last], axis=1)], axis=0
        )
        rows[c] = own + added
        if c == 0:
            kv_copy.wait()
        attend(c)
        flat_res = res[c].reshape(flat, HD).astype(BF16)
        answer = dot(y_pick, flat_res).astype(BF16)
        answer = yield from swap(answer, ys, yr, ys_sem, yr_sem, c)
        merged = jnp.where(f_moved, dot(y_in, answer), flat_res.astype(F32)).astype(BF16)
        for m in range(cap):
            chosen = pick(jnp.where(p_index < 0, -1, p_base + m), flat)
            back[c, :, :, m * HD : (m + 1) * HD] = (
                dot(chosen, merged).astype(BF16).reshape(n, HEADS, HD)
            )
        send_all(back, home, back_sem, home_sem, c)
        yield

    running = [work(c) for c in range(CHUNKS)]
    while running:
        for w in list(running):
            if next(w, running) is running:
                running.remove(w)

    j_hit = iota((flat, n_rows), 1) == f_k
    eye = iota((n_rows, n_rows), 0) == iota((n_rows, n_rows), 1)
    owner_row = row_sum(eye, owner)
    place_row = row_sum(eye, place)
    out_from = lane_sum(j_hit, owner_row) * HEADS + f_head
    out_place = lane_sum(j_hit, place_row)
    chosen = [pick(jnp.where(out_place == m, out_from, -1), n * HEADS) for m in range(cap)]
    for c in range(CHUNKS):
        wait_recv(back, home, back_sem, home_sem, c)
        got = home[c].reshape(n * HEADS, cap * HD)
        total = sum(dot(chosen[m], got[:, m * HD : (m + 1) * HD]) for m in range(cap)).astype(BF16)
        for h in range(HEADS):
            lanes = slice((c * HEADS + h) * HD, (c * HEADS + h + 1) * HD)
            out_ref[:, lanes] = total[h * n_rows : (h + 1) * n_rows]
    for c in range(CHUNKS):
        wait_send(send, recv, send_sem, recv_sem, c)
        wait_send(back, home, back_sem, home_sem, c)


def on_device(
    kv_cache, draft_rows, cache_lengths, row_offsets, draft_order, pair_mask, moved_slots
):
    n = lax.axis_size("req")
    n_rows = draft_rows.shape[0]
    cap = n_rows // row_offsets.shape[0]
    block = -(-PARTS * cap // 16) * 16
    swaps = sum(values - 1 for _, values in digits_of(n))
    x_shape = (CHUNKS, swaps, 4 * DRAFT, PART_W + HD)
    y_shape = (CHUNKS, swaps, HEADS * DRAFT, HD)
    vmem, smem = pltpu.VMEM, pltpu.SMEM
    dma = pltpu.SemaphoreType.DMA
    return pl.pallas_call(
        functools.partial(kernel, n, cap),
        out_shape=jax.ShapeDtypeStruct((n_rows, QW), BF16),
        in_specs=[pl.BlockSpec(memory_space=smem)] * 3
        + [pl.BlockSpec(memory_space=vmem)] * 3
        + [pl.BlockSpec(memory_space=pl.ANY)],
        out_specs=pl.BlockSpec(memory_space=vmem),
        scratch_shapes=[
            vmem(kv_cache.shape, BF16),
            vmem((CHUNKS, n, block, PART_W), BF16),
            vmem((CHUNKS, n, block, PART_W), BF16),
            vmem((CHUNKS, PARTS * n_rows, PART_W), F32),
            vmem((CHUNKS, HEADS, n_rows, HD), F32),
            vmem((CHUNKS, n, HEADS, cap * HD), BF16),
            vmem((CHUNKS, n, HEADS, cap * HD), BF16),
            vmem(x_shape, BF16),
            vmem(x_shape, BF16),
            vmem(y_shape, BF16),
            vmem(y_shape, BF16),
            dma,
            dma((CHUNKS, n)), dma((CHUNKS, n)), dma((CHUNKS, n)), dma((CHUNKS, n)),
            dma((CHUNKS, swaps)), dma((CHUNKS, swaps)), dma((CHUNKS, swaps)), dma((CHUNKS, swaps)),
        ],
        compiler_params=pltpu.CompilerParams(
            collective_id=0, has_side_effects=True, vmem_limit_bytes=56 * 1024 * 1024
        ),
    )(
        cache_lengths, pair_mask, moved_slots, draft_order.reshape(1, n_rows),
        row_offsets.reshape(1, row_offsets.shape[0]), draft_rows, kv_cache,
    )


def solution(mesh):
    in_specs = (
        P(("groups", "req"), None, None, None),
        P(("groups", "req"), None),
        P("groups"),
        P("groups"),
        P(("groups", "req")),
        P("groups"),
        P("groups"),
    )
    out_specs = P(("groups", "req"), None)
    return jax.shard_map(
        on_device, mesh=mesh, in_specs=in_specs, out_specs=out_specs, check_vma=False
    )
```

time: 108 us -> 56.3 us (0.52)
  Pallas kernels: 0 us -> 53.7 us
  local copies, waits for them, and re-layouts: 30.1 us -> 1.77 us
  waiting for transfers between devices: 24.9 us -> 0 us
  blocking collectives: 18.5 us -> 0 us
  starting transfers between devices: 17.5 us -> 0 us
  matrix products: 9.96 us -> 0 us
  other arithmetic: 3.14 us -> 0 us
  between operations: 2.85 us -> 0.66 us
    pallas_call x0 -> x1, Pallas kernels: none -> 53.7 us  [on_device(): pl.pallas_call(functools.partial(kernel, n, cap), out_shape=jax.ShapeDtyp...]
    all_to_all x1 -> x0, blocking collectives: 18.5 us -> none  [on_device(): lax.all_to_all(backward, 'req', split_axis=0, concat_axis=0, tiled=True)]
    another operation x2 -> x0, local copies, waits for them, and re-layouts: 15.4 us -> none  [the longest x1 7.73 us: attend_slots(): cache_vals = page_pool[:, :, 1].reshape(slots, span, KVH, HD)]
    all_to_all x1 -> x0, waiting for transfers between devices: 13.2 us -> none  [on_device(): lax.all_to_all(outgoing, 'req', split_axis=0, concat_axis=0, tiled=True)]
    ppermute x8 -> x0, waiting for transfers between devices: 11.6 us -> none  [from_partner(): lax.ppermute(value, axis, [(i, i ^ 1 << apart) for i in range(lax.axis_si...]
    ppermute x8 -> x0, starting transfers between devices: 10.2 us -> none  [from_partner(): lax.ppermute(value, axis, [(i, i ^ 1 << apart) for i in range(lax.axis_si...]
    dot_general x8 -> x0, matrix products: 9.96 us -> none  [the longest x1 4.34 us: attend_slots(): jnp.einsum('rtghd,rlgd->rtghl', queries, cache_keys, preferred_element_ty...]
    all_to_all x1 -> x0, starting transfers between devices: 7.37 us -> none  [on_device(): lax.all_to_all(outgoing, 'req', split_axis=0, concat_axis=0, tiled=True)]
  transfers between devices with their start and end apart: 9 -> 0, of which waited for: 7 -> 0; matrix products, arithmetic and copies ran while one was open for 24% -> 0% of each run, Pallas kernels for 0% -> 0%
where the time goes in v1:
time: 56.3 us; the launch traced here: 56.1 us
  Pallas kernels  53.7 us (95%)
  local copies, waits for them, and re-layouts  1.77 us (3%)
  between operations  0.66 us (1%)
    pallas_call x1, Pallas kernels, on_device(): pl.pallas_call(functools.partial(kernel, n, cap), out_shape=jax.ShapeDtyp...  53.7 us
    unnamed x1, local copies, waits for them, and re-layouts  1.77 us

profile of v1, /device:TPU:0, one launch (start us, length us, event | category | flops | bytes accessed | tf_op | source)
XLA Modules:
  0.0 56.1 jit_solution(2889851927500228726)
XLA Ops:
  0.7 53.7 %shard_map.73 = bf16[48,4096]{1,0:T(8,128)(2,1)} custom-call(s32[192]{0:T(256)} %lengths.1, s32[1]{0:T(128)S(6)} %copy.9.mask, s32[16]{0:T(128)} %moved.1, s32[1,48]{1,0:T(1,128)} %bitcast.2, s32[1,16]{1,0:T(1,128)} %bitcast.3, bf16[48,5120]{1,0:T(8,128)(2,1)} %draft_ref.1, bf16[36,2,128,512]{3,2,1,0:T(8,128)(2,1)} %kv_hbm.1), custom_call_target="tpu_custom_call" | custom-call | tf_op jit(solution)/shard_map/pallas_call | solution.py:350
  54.4 1.8 %copy.10 = bf16[48,4096]{1,0:T(8,128)(2,1)} copy(bf16[48,4096]{1,0:T(8,128)(2,1)} %shard_map.73) | data formatting | bytes 786432

commit v2 on v1

--- a/solution.py
+++ b/solution.py
@@ -81,7 +81,8 @@
 
 def kernel(
     n, cap, lengths, mask, moved, order_ref, off_ref, draft_ref, kv_hbm, out_ref,
-    kv, send, recv, rows, res, back, home, xs, xr, ys, yr,
+    kv, send, recv, rows, res, partial, back, home, xs, xr, ys, yr,
+    unpack, x_pick, back_pick, y_pick, out_pick,
     kv_sem, send_sem, recv_sem, back_sem, home_sem, xs_sem, xr_sem, ys_sem, yr_sem,
 ):
     me = lax.axis_index("req")
@@ -171,165 +172,211 @@
     off_col = lane_sum(iota((wide, n_off), 1) == small_div(k_col, cap), off)
     source = wrap(me + off_col, n)
     from_col = source * block + small_div(r_col, n_rows) * cap + small_mod(k_col, cap)
-    is_moved = lax.shift_right_logical(k_col, 2) == my_slot
-    unpack = pick(jnp.where(is_moved, -1, from_col), n * block)
+    unpack[...] = pick(from_col, n * block)
     x_row = iota((4 * DRAFT, 1), 0)
     x_draft = small_mod(x_row, DRAFT)
     x_k = my_slot * DRAFT + x_draft
     x_off = lane_sum(iota((4 * DRAFT, n_off), 1) == small_div(x_k, cap), off)
     x_from = wrap(me + x_off, n) * block + small_mod(x_k, cap)
     x_tile = small_div(x_row, DRAFT)
-    x_pick = pick(x_from + x_tile * cap, n * block)
-    x_last = [pick(jnp.where(x_tile == i, x_from + Q_PARTS * cap, -1), n * block) for i in range(4)]
-    q_rows = Q_PARTS * n_rows
-    x_in = pick(
-        jnp.where(is_moved, small_div(r_col, n_rows) * DRAFT + small_mod(k_col, DRAFT), -1)[:q_rows],
-        4 * DRAFT,
-    )
-    last_moved = is_moved[q_rows:]
-    last_draft = small_mod(k_col, DRAFT)[q_rows:]
-    x_in_last = [pick(jnp.where(last_moved, i * DRAFT + last_draft, -1), 4 * DRAFT) for i in range(4)]
+    x_pick[:, : n * block] = pick(x_from + x_tile * cap, n * block)
+    for i in range(4):
+        x_pick[:, (1 + i) * n * block : (2 + i) * n * block] = pick(
+            jnp.where(x_tile == i, x_from + Q_PARTS * cap, -1), n * block
+        )
     flat = HEADS * n_rows
-    y_row = iota((HEADS * DRAFT, 1), 0)
-    y_pick = pick(
-        small_div(y_row, DRAFT) * n_rows + my_slot * DRAFT + small_mod(y_row, DRAFT), flat
-    )
-    f_row = iota((flat, 1), 0)
-    f_k = small_mod(f_row, n_rows)
-    f_head = small_div(f_row, n_rows)
-    f_moved = lax.shift_right_logical(f_k, 2) == my_slot
-    y_in = pick(f_head * DRAFT + small_mod(f_k, DRAFT), HEADS * DRAFT)
     p_row = iota((n * HEADS, 1), 0)
     p_peer = small_div(p_row, HEADS)
-    p_hit = p_peer == wrap(me + off, n)
-    p_index = lane_sum(p_hit, iota((1, n_off), 1) + 1) - 1
-    p_base = small_mod(p_row, HEADS) * n_rows + p_index * cap
-
-    def swap(cur, s_ref, r_ref, s_sem, r_sem, c):
-        slot = 0
-        for shift, values in digits:
-            s_ref[c, slot] = cur
-            copies = []
-            for delta in range(1, values):
-                copies.append(
-                    pltpu.make_async_remote_copy(
-                        src_ref=s_ref.at[c, slot], dst_ref=r_ref.at[c, slot + delta - 1],
-                        send_sem=s_sem.at[c, slot + delta - 1],
-                        recv_sem=r_sem.at[c, slot + delta - 1],
-                        device_id={"req": flip(me, delta << shift)}, device_id_type=MESH,
-                    )
+    p_head = small_mod(p_row, HEADS)
+    p_index = lane_sum(p_peer == wrap(me + off, n), iota((1, n_off), 1) + 1) - 1
+    y_base = (
+        small_div(p_head, GRP) * GRP * DRAFT
+        + small_mod(p_head, PART_HEADS) * 2 * DRAFT
+        + small_mod(small_div(p_head, PART_HEADS), 2) * DRAFT
+    )
+    for m in range(cap):
+        p_k = p_index * cap + m
+        p_moved = lax.shift_right_arithmetic(p_k, 2) == my_slot
+        stays = (p_index >= 0) & jnp.logical_not(p_moved)
+        back_pick[m] = pick(jnp.where(stays, p_head * n_rows + p_k, -1), flat)
+        y_pick[m] = pick(jnp.where(p_moved, y_base + p_k - my_slot * DRAFT, -1), HEADS * DRAFT)
+    f_row = iota((flat, 1), 0)
+    j_hit = iota((flat, n_rows), 1) == small_mod(f_row, n_rows)
+    eye = iota((n_rows, n_rows), 0) == iota((n_rows, n_rows), 1)
+    out_from = lane_sum(j_hit, row_sum(eye, owner)) * HEADS + small_div(f_row, n_rows)
+    out_place = lane_sum(j_hit, row_sum(eye, place))
+    for m in range(cap):
+        out_pick[m] = pick(jnp.where(out_place == m, out_from, -1), n * HEADS)
+
+    class Swap:
+        def __init__(self, cur, s_ref, r_ref, s_sem, r_sem, c):
+            self.cur, self.refs, self.c = cur, (s_ref, r_ref, s_sem, r_sem), c
+            self.slot, self.todo = 0, list(digits)
+            self.start()
+
+        def start(self):
+            s_ref, r_ref, s_sem, r_sem = self.refs
+            shift, values = self.todo[0]
+            c, slot = self.c, self.slot
+            s_ref[c, slot] = self.cur
+            self.copies = [
+                pltpu.make_async_remote_copy(
+                    src_ref=s_ref.at[c, slot], dst_ref=r_ref.at[c, slot + delta - 1],
+                    send_sem=s_sem.at[c, slot + delta - 1],
+                    recv_sem=r_sem.at[c, slot + delta - 1],
+                    device_id={"req": flip(me, delta << shift)}, device_id_type=MESH,
                 )
-                copies[-1].start()
-            yield
+                for delta in range(1, values)
+            ]
+            for copy in self.copies:
+                copy.start()
+
+        def receive(self):
+            r_ref = self.refs[1]
+            shift, values = self.todo.pop(0)
             digit = jnp.bitwise_and(jnp.right_shift(pair, shift), values - 1)
             for delta in range(1, values):
-                copies[delta - 1].wait()
-                cur = jnp.where(digit == delta, r_ref[c, slot + delta - 1], cur)
-            slot += values - 1
-        return cur
-
-    half = DRAFT
+                self.copies[delta - 1].wait()
+                self.cur = jnp.where(digit == delta, r_ref[self.c, self.slot + delta - 1], self.cur)
+            self.slot += values - 1
+
+        def step(self):
+            self.receive()
+            if self.todo:
+                self.start()
+
+        def finish(self):
+            while self.todo:
+                self.step()
+            return self.cur
+
     rows_p = 2 * DRAFT
     span = PPR * PAGE
     factor = 1.0 / jnp.sqrt(F32(HD))
     block_row = small_mod(iota((GRP * rows_p, 1), 0), rows_p)
-    first = block_row < half
+    first = block_row < DRAFT
     n_col = iota((GRP * rows_p, rows_p), 1)
     new_ok = (lax.shift_right_logical(n_col, 2) == lax.shift_right_logical(block_row, 2)) & (
         n_col <= block_row
     )
     position = iota((GRP * rows_p, span), 1)
 
-    def attend(c):
-        def body(pr, carry):
-            at = pl.multiple_of(pr * rows_p, rows_p)
+    def cached(slot, which, c, g):
+        lanes = slice((c * KV_HERE + g) * HD, (c * KV_HERE + g + 1) * HD)
+        return kv[pl.ds(slot * PPR, PPR), which, :, lanes].reshape(span, HD)
+
+    def weigh(score, ok, new_score, new_ok):
+        score = jnp.where(ok, score * factor, -1e30)
+        new_score = jnp.where(new_ok, new_score * factor, -1e30)
+        peak = jnp.maximum(
+            jnp.max(score, axis=1, keepdims=True), jnp.max(new_score, axis=1, keepdims=True)
+        )
+        w = jnp.where(ok, jnp.exp(score - peak), 0.0)
+        new_w = jnp.where(new_ok, jnp.exp(new_score - peak), 0.0)
+        total = jnp.sum(w, axis=1, keepdims=True) + jnp.sum(new_w, axis=1, keepdims=True)
+        return w.astype(BF16), new_w.astype(BF16), total
+
+    def attend(c, g):
+        for pr in range(R_DEV // 2):
+            at = pr * rows_p
             slot = pr * 2
             limit = jnp.where(first, lengths[me * R_DEV + slot], lengths[me * R_DEV + slot + 1])
-            ok = position < limit
-
-            def cached(which, g):
-                lanes = slice((c * KV_HERE + g) * HD, (c * KV_HERE + g + 1) * HD)
-                return jnp.concatenate(
-                    [kv[pl.ds((slot + a) * PPR, PPR), which, :, lanes].reshape(span, HD) for a in (0, 1)],
-                    axis=1,
-                )
-
-            for g in range(KV_HERE):
-                tiles = []
-                for h in range(GRP):
-                    p, i = divmod(g * GRP + h, PART_HEADS)
-                    tiles.append(rows[c, pl.ds(p * n_rows + at, rows_p), i * HD : (i + 1) * HD])
-                q = jnp.concatenate(tiles, axis=0)
-                last = pl.ds(Q_PARTS * n_rows + at, rows_p)
-                new_k = rows[c, last, g * HD : (g + 1) * HD].astype(BF16)
-                new_v = rows[c, last, (KV_HERE + g) * HD : (KV_HERE + g + 1) * HD].astype(BF16)
-                q2 = jnp.concatenate([jnp.where(first, q, 0.0), jnp.where(first, 0.0, q)], axis=1)
-                score = dot_t(q2.astype(BF16), cached(0, g)) * factor
-                new_score = dot_t(q.astype(BF16), new_k) * factor
-                score = jnp.where(ok, score, -1e30)
-                new_score = jnp.where(new_ok, new_score, -1e30)
-                peak = jnp.maximum(
-                    jnp.max(score, axis=1, keepdims=True), jnp.max(new_score, axis=1, keepdims=True)
-                )
-                w = jnp.where(ok, jnp.exp(score - peak), 0.0)
-                new_w = jnp.where(new_ok, jnp.exp(new_score - peak), 0.0)
-                total = jnp.sum(w, axis=1, keepdims=True) + jnp.sum(new_w, axis=1, keepdims=True)
-                both = dot(w.astype(BF16), cached(1, g))
-                out = jnp.where(first, both[:, :HD], both[:, HD:]) + dot(new_w.astype(BF16), new_v)
-                out = (out / total).reshape(GRP, rows_p, HD)
-                res[c, g * GRP : (g + 1) * GRP, pl.ds(at, rows_p), :] = out
-            return carry
-
-        lax.fori_loop(0, R_DEV // 2, body, 0)
-
-    def work(c):
+            both = [
+                jnp.concatenate([cached(slot + a, which, c, g) for a in (0, 1)], axis=1)
+                for which in (0, 1)
+            ]
+            tiles = []
+            for h in range(GRP):
+                p, i = divmod(g * GRP + h, PART_HEADS)
+                r0 = p * n_rows + at
+                tiles.append(rows[c, r0 : r0 + rows_p, i * HD : (i + 1) * HD])
+            q = jnp.concatenate(tiles, axis=0)
+            r0 = Q_PARTS * n_rows + at
+            new_k = rows[c, r0 : r0 + rows_p, g * HD : (g + 1) * HD].astype(BF16)
+            new_v = rows[c, r0 : r0 + rows_p, (KV_HERE + g) * HD : (KV_HERE + g + 1) * HD].astype(BF16)
+            q2 = jnp.concatenate([jnp.where(first, q, 0.0), jnp.where(first, 0.0, q)], axis=1)
+            w, new_w, total = weigh(
+                dot_t(q2.astype(BF16), both[0]), position < limit, dot_t(q.astype(BF16), new_k), new_ok
+            )
+            out = dot(w, both[1])
+            out = jnp.where(first, out[:, :HD], out[:, HD:]) + dot(new_w, new_v)
+            res[c, g * GRP : (g + 1) * GRP, at : at + rows_p, :] = (out / total).reshape(
+                GRP, rows_p, HD
+            )
+
+    v_rows = GRP * DRAFT
+    v_row = iota((v_rows, 4 * DRAFT), 0)
+    v_col = iota((v_rows, 4 * DRAFT), 1)
+    v_position = iota((v_rows, span), 1)
+
+    def attend_visitor(c, visitor):
+        v = visitor.astype(F32)
+        tail = v[:, PART_W:]
+        new_k = tail.astype(BF16)
+        new_v = jnp.concatenate([tail[2 * DRAFT :], tail[: 2 * DRAFT]], axis=0).astype(BF16)
+        ok = v_position < lengths[me * R_DEV + my_slot]
+        outs = []
+        for g in range(KV_HERE):
+            q = jnp.concatenate(
+                [v[g * 2 * DRAFT : (g + 1) * 2 * DRAFT, i * HD : (i + 1) * HD] for i in range(PART_HEADS)],
+                axis=0,
+            ).astype(BF16)
+            seen = (small_div(v_col, DRAFT) == g) & (small_mod(v_col, DRAFT) <= small_mod(v_row, DRAFT))
+            w, new_w, total = weigh(
+                dot_t(q, cached(my_slot, 0, c, g)), ok, dot_t(q, new_k), seen
+            )
+            outs.append((dot(w, cached(my_slot, 1, c, g)) + dot(new_w, new_v)) / total)
+        return jnp.concatenate(outs, axis=0).astype(BF16)
+
+    def arrive(c):
         wait_recv(send, recv, send_sem, recv_sem, c)
         got = recv[c].reshape(n * block, PART_W)
-        last = sum(dot(x_last[i], got[:, i * HD : (i + 1) * HD]) for i in range(4))
-        mine = jnp.concatenate([dot(x_pick, got), last], axis=1).astype(BF16)
-        own = dot(unpack, got)
-        visitor = yield from swap(mine, xs, xr, xs_sem, xr_sem, c)
-        tail = visitor[:, PART_W:]
-        added = jnp.concatenate(
-            [dot(x_in, visitor[:, :PART_W]),
-             jnp.concatenate([dot(m, tail) for m in x_in_last], axis=1)], axis=0
-        )
-        rows[c] = own + added
-        if c == 0:
-            kv_copy.wait()
-        attend(c)
+        stack = jnp.concatenate([got[:, i * HD : (i + 1) * HD] for i in range(4)], axis=0)
+        mine = jnp.concatenate(
+            [dot(x_pick[:, : n * block], got), dot(x_pick[:, n * block :], stack)], axis=1
+        ).astype(BF16)
+        x_swap = Swap(mine, xs, xr, xs_sem, xr_sem, c)
+        rows[c] = dot(unpack[...], got)
+        return x_swap
+
+    def pack_back(c):
         flat_res = res[c].reshape(flat, HD).astype(BF16)
-        answer = dot(y_pick, flat_res).astype(BF16)
-        answer = yield from swap(answer, ys, yr, ys_sem, yr_sem, c)
-        merged = jnp.where(f_moved, dot(y_in, answer), flat_res.astype(F32)).astype(BF16)
         for m in range(cap):
-            chosen = pick(jnp.where(p_index < 0, -1, p_base + m), flat)
-            back[c, :, :, m * HD : (m + 1) * HD] = (
-                dot(chosen, merged).astype(BF16).reshape(n, HEADS, HD)
-            )
+            partial[c, :, m * HD : (m + 1) * HD] = dot(back_pick[m], flat_res)
+
+    def send_back(c, answer):
+        for m in range(cap):
+            lanes = slice(m * HD, (m + 1) * HD)
+            total = partial[c, :, lanes] + dot(y_pick[m], answer)
+            back[c, :, :, lanes] = total.astype(BF16).reshape(n, HEADS, HD)
         send_all(back, home, back_sem, home_sem, c)
-        yield
-
-    running = [work(c) for c in range(CHUNKS)]
-    while running:
-        for w in list(running):
-            if next(w, running) is running:
-                running.remove(w)
-
-    j_hit = iota((flat, n_rows), 1) == f_k
-    eye = iota((n_rows, n_rows), 0) == iota((n_rows, n_rows), 1)
-    owner_row = row_sum(eye, owner)
-    place_row = row_sum(eye, place)
-    out_from = lane_sum(j_hit, owner_row) * HEADS + f_head
-    out_place = lane_sum(j_hit, place_row)
-    chosen = [pick(jnp.where(out_place == m, out_from, -1), n * HEADS) for m in range(cap)]
-    for c in range(CHUNKS):
+
+    def finish(c):
         wait_recv(back, home, back_sem, home_sem, c)
         got = home[c].reshape(n * HEADS, cap * HD)
-        total = sum(dot(chosen[m], got[:, m * HD : (m + 1) * HD]) for m in range(cap)).astype(BF16)
+        total = sum(dot(out_pick[m], got[:, m * HD : (m + 1) * HD]) for m in range(cap)).astype(BF16)
         for h in range(HEADS):
             lanes = slice((c * HEADS + h) * HD, (c * HEADS + h + 1) * HD)
             out_ref[:, lanes] = total[h * n_rows : (h + 1) * n_rows]
+
+    x0 = arrive(0)
+    kv_copy.wait()
+    attend(0, 0)
+    x0.step()
+    attend(0, 1)
+    x1 = arrive(1)
+    y0 = Swap(attend_visitor(0, x0.finish()), ys, yr, ys_sem, yr_sem, 0)
+    attend(1, 0)
+    x1.step()
+    y0.step()
+    attend(1, 1)
+    pack_back(0)
+    send_back(0, y0.finish())
+    y1 = Swap(attend_visitor(1, x1.finish()), ys, yr, ys_sem, yr_sem, 1)
+    pack_back(1)
+    send_back(1, y1.finish())
+    finish(0)
+    finish(1)
     for c in range(CHUNKS):
         wait_send(send, recv, send_sem, recv_sem, c)
         wait_send(back, home, back_sem, home_sem, c)
@@ -360,12 +407,18 @@
             vmem((CHUNKS, n, block, PART_W), BF16),
             vmem((CHUNKS, PARTS * n_rows, PART_W), F32),
             vmem((CHUNKS, HEADS, n_rows, HD), F32),
+            vmem((CHUNKS, n * HEADS, cap * HD), F32),
             vmem((CHUNKS, n, HEADS, cap * HD), BF16),
             vmem((CHUNKS, n, HEADS, cap * HD), BF16),
             vmem(x_shape, BF16),
             vmem(x_shape, BF16),
             vmem(y_shape, BF16),
             vmem(y_shape, BF16),
+            vmem((PARTS * n_rows, n * block), BF16),
+            vmem((4 * DRAFT, 5 * n * block), BF16),
+            vmem((cap, n * HEADS, HEADS * n_rows), BF16),
+            vmem((cap, n * HEADS, HEADS * DRAFT), BF16),
+            vmem((cap, HEADS * n_rows, n * HEADS), BF16),
             dma,
             dma((CHUNKS, n)), dma((CHUNKS, n)), dma((CHUNKS, n)), dma((CHUNKS, n)),
             dma((CHUNKS, swaps)), dma((CHUNKS, swaps)), dma((CHUNKS, swaps)), dma((CHUNKS, swaps)),

time: 56.3 us -> 53 us (0.941)
  Pallas kernels: 53.7 us -> 50.3 us
    pallas_call x1, Pallas kernels: 53.7 us -> 50.3 us  [on_device(): pl.pallas_call(functools.partial(kernel, n, cap), out_shape=jax.ShapeDtyp...]
where the time goes in v2:
time: 53 us; the launch traced here: 52.8 us
  Pallas kernels  50.3 us (95%)
  local copies, waits for them, and re-layouts  1.77 us (3%)
  between operations  0.66 us (1%)
    pallas_call x1, Pallas kernels, on_device(): pl.pallas_call(functools.partial(kernel, n, cap), out_shape=jax.ShapeDtyp...  50.3 us
    unnamed x1, local copies, waits for them, and re-layouts  1.77 us

profile of v2, /device:TPU:0, one launch (start us, length us, event | category | flops | bytes accessed | tf_op | source)
XLA Modules:
  0.0 52.8 jit_solution(10949738714608625255)
XLA Ops:
  0.7 50.3 %shard_map.73 = bf16[48,4096]{1,0:T(8,128)(2,1)} custom-call(s32[192]{0:T(256)} %lengths.1, s32[1]{0:T(128)S(6)} %copy.9.mask, s32[16]{0:T(128)} %moved.1, s32[1,48]{1,0:T(1,128)} %bitcast.2, s32[1,16]{1,0:T(1,128)} %bitcast.3, bf16[48,5120]{1,0:T(8,128)(2,1)} %draft_ref.1, bf16[36,2,128,512]{3,2,1,0:T(8,128)(2,1)} %kv_hbm.1), custom_call_target="tpu_custom_call" | custom-call | tf_op jit(solution)/shard_map/pallas_call | solution.py:397
  51.0 1.8 %copy.10 = bf16[48,4096]{1,0:T(8,128)(2,1)} copy(bf16[48,4096]{1,0:T(8,128)(2,1)} %shard_map.73) | data formatting | bytes 786432

commit v3 on v2

--- a/solution.py
+++ b/solution.py
@@ -90,21 +90,34 @@
     block = send.shape[2]
     n_off = off_ref.shape[1]
     digits = digits_of(n)
+    cuts = [1 + (n - 1) * i // 4 for i in (1, 2, 3)]
 
     kv_copy = pltpu.make_async_copy(kv_hbm, kv, kv_sem)
     kv_copy.start()
 
-    def peer_of(i):
-        step = (i + n // 2 - 1) % (n - 1) + 1
-        return (me + step) % n
+    bits = n.bit_length() - 1
+    turn = [(1 << b) * (1 - 2 * ((me // (1 << b)) % 2)) for b in range(bits)]
+
+    def each_peer(body, lo=1, hi=n):
+        def one(i, carry):
+            peer = me
+            for b in range(bits):
+                peer = peer + turn[b] * ((i // (1 << (bits - 1 - b))) % 2)
+            body(peer)
+            return carry
+
+        if n <= 16:
+            for i in range(lo, hi):
+                one(i, 0)
+        else:
+            lax.fori_loop(lo, hi, one, 0)
 
     barrier = pltpu.get_barrier_semaphore()
-
-    def greet(i, carry):
-        pl.semaphore_signal(barrier, inc=1, device_id={"req": peer_of(i)}, device_id_type=MESH)
-        return carry
-
-    lax.fori_loop(0, n - 1, greet, 0)
+    each_peer(
+        lambda peer: pl.semaphore_signal(
+            barrier, inc=1, device_id={"req": peer}, device_id_type=MESH
+        )
+    )
 
     order = order_ref[...]
     off = off_ref[...]
@@ -126,32 +139,26 @@
             device_id={"req": peer}, device_id_type=MESH,
         )
 
-    def send_all(s_ref, r_ref, s_sem, r_sem, c):
-        def body(i, carry):
-            exchange(s_ref, r_ref, s_sem, r_sem, c, peer_of(i)).start()
-            return carry
-
-        lax.fori_loop(0, n - 1, body, 0)
-        r_ref[c, me] = s_ref[c, me]
+    def send_some(s_ref, r_ref, s_sem, r_sem, c, lo, hi):
+        each_peer(lambda peer: exchange(s_ref, r_ref, s_sem, r_sem, c, peer).start(), lo, hi)
 
     def wait_recv(s_ref, r_ref, s_sem, r_sem, c):
-        def body(i, carry):
-            src = peer_of(i)
-            pltpu.make_async_remote_copy(
+        each_peer(
+            lambda src: pltpu.make_async_remote_copy(
                 src_ref=s_ref.at[c, src], dst_ref=r_ref.at[c, src],
                 send_sem=s_sem.at[c, src], recv_sem=r_sem.at[c, src],
                 device_id={"req": src}, device_id_type=MESH,
             ).wait_recv()
-            return carry
-
-        lax.fori_loop(0, n - 1, body, 0)
+        )
 
     def wait_send(s_ref, r_ref, s_sem, r_sem, c):
-        def body(i, carry):
-            exchange(s_ref, r_ref, s_sem, r_sem, c, peer_of(i)).wait_send()
-            return carry
-
-        lax.fori_loop(0, n - 1, body, 0)
+        each_peer(lambda peer: exchange(s_ref, r_ref, s_sem, r_sem, c, peer).wait_send())
+
+    def send_rows(c, lo, hi):
+        send_some(send, recv, send_sem, recv_sem, c, lo, hi)
+
+    def send_answers(c, lo, hi):
+        send_some(back, home, back_sem, home_sem, c, lo, hi)
 
     for c in range(CHUNKS):
         q0 = c * HEADS * HD
@@ -163,7 +170,9 @@
         send[c] = dot(pack, stacked).astype(BF16).reshape(n, block, PART_W)
         if c == 0:
             pl.semaphore_wait(barrier, n - 1)
-        send_all(send, recv, send_sem, recv_sem, c)
+            send_rows(0, 1, n)
+        recv[c, me] = send[c, me]
+    send_rows(1, 1, cuts[0])
 
     my_slot = moved[me]
     pair = mask[0]
@@ -349,32 +358,39 @@
             lanes = slice(m * HD, (m + 1) * HD)
             total = partial[c, :, lanes] + dot(y_pick[m], answer)
             back[c, :, :, lanes] = total.astype(BF16).reshape(n, HEADS, HD)
-        send_all(back, home, back_sem, home_sem, c)
+        home[c, me] = back[c, me]
 
     def finish(c):
         wait_recv(back, home, back_sem, home_sem, c)
         got = home[c].reshape(n * HEADS, cap * HD)
         total = sum(dot(out_pick[m], got[:, m * HD : (m + 1) * HD]) for m in range(cap)).astype(BF16)
         for h in range(HEADS):
-            lanes = slice((c * HEADS + h) * HD, (c * HEADS + h + 1) * HD)
-            out_ref[:, lanes] = total[h * n_rows : (h + 1) * n_rows]
+            out_ref[c * HEADS + h] = total[h * n_rows : (h + 1) * n_rows]
 
     x0 = arrive(0)
+    send_rows(1, cuts[0], cuts[1])
     kv_copy.wait()
     attend(0, 0)
     x0.step()
+    send_rows(1, cuts[1], cuts[2])
     attend(0, 1)
+    y0 = Swap(attend_visitor(0, x0.finish()), ys, yr, ys_sem, yr_sem, 0)
+    send_rows(1, cuts[2], n)
+    pack_back(0)
+    y0.step()
     x1 = arrive(1)
-    y0 = Swap(attend_visitor(0, x0.finish()), ys, yr, ys_sem, yr_sem, 0)
     attend(1, 0)
     x1.step()
-    y0.step()
+    send_back(0, y0.finish())
+    send_answers(0, 1, cuts[1])
     attend(1, 1)
-    pack_back(0)
-    send_back(0, y0.finish())
     y1 = Swap(attend_visitor(1, x1.finish()), ys, yr, ys_sem, yr_sem, 1)
+    send_answers(0, cuts[1], cuts[2])
     pack_back(1)
+    y1.step()
+    send_answers(0, cuts[2], n)
     send_back(1, y1.finish())
+    send_answers(1, 1, n)
     finish(0)
     finish(1)
     for c in range(CHUNKS):
@@ -394,9 +410,9 @@
     y_shape = (CHUNKS, swaps, HEADS * DRAFT, HD)
     vmem, smem = pltpu.VMEM, pltpu.SMEM
     dma = pltpu.SemaphoreType.DMA
-    return pl.pallas_call(
+    heads_first = pl.pallas_call(
         functools.partial(kernel, n, cap),
-        out_shape=jax.ShapeDtypeStruct((n_rows, QW), BF16),
+        out_shape=jax.ShapeDtypeStruct((QW // HD, n_rows, HD), BF16),
         in_specs=[pl.BlockSpec(memory_space=smem)] * 3
         + [pl.BlockSpec(memory_space=vmem)] * 3
         + [pl.BlockSpec(memory_space=pl.ANY)],
@@ -430,6 +446,7 @@
         cache_lengths, pair_mask, moved_slots, draft_order.reshape(1, n_rows),
         row_offsets.reshape(1, row_offsets.shape[0]), draft_rows, kv_cache,
     )
+    return heads_first.transpose(1, 0, 2).reshape(n_rows, QW)
 
 
 def solution(mesh):

time: 53 us -> 54.6 us (1.030)
  Pallas kernels: 50.3 us -> 51.9 us
    reshape x0 -> x1, local copies, waits for them, and re-layouts: none -> 1.77 us  [on_device(): return heads_first.transpose(1, 0, 2).reshape(n_rows, QW)]
    unnamed x1 -> x0, local copies, waits for them, and re-layouts: 1.77 us -> none
    pallas_call x1, Pallas kernels: 50.3 us -> 51.9 us  [on_device(): pl.pallas_call(functools.partial(kernel, n, cap), out_shape=jax.ShapeDtyp...]
where the time goes in v3:
time: 54.6 us; the launch traced here: 54.3 us
  Pallas kernels  51.9 us (95%)
  local copies, waits for them, and re-layouts  1.77 us (3%)
  between operations  0.66 us (1%)
    pallas_call x1, Pallas kernels, on_device(): pl.pallas_call(functools.partial(kernel, n, cap), out_shape=jax.ShapeDtyp...  51.9 us
    reshape x1, local copies, waits for them, and re-layouts, on_device(): return heads_first.transpose(1, 0, 2).reshape(n_rows, QW)  1.77 us

profile of v3, /device:TPU:0, one launch (start us, length us, event | category | flops | bytes accessed | tf_op | source)
XLA Modules:
  0.0 54.3 jit_solution(15233758713705274336)
XLA Ops:
  0.7 51.9 %shard_map.73 = bf16[32,48,128]{2,1,0:T(8,128)(2,1)} custom-call(s32[192]{0:T(256)} %lengths.1, s32[1]{0:T(128)S(6)} %copy.11.mask, s32[16]{0:T(128)} %moved.1, s32[1,48]{1,0:T(1,128)} %bitcast.8, s32[1,16]{1,0:T(1,128)} %bitcast.9, bf16[48,5120]{1,0:T(8,128)(2,1)} %draft_ref.1, bf16[36,2,128,512]{3,2,1,0:T(8,128)(2,1)} %kv_hbm.1), custom_call_target="tpu_custom_call" | custom-call | tf_op jit(solution)/shard_map/pallas_call | solution.py:413
  52.6 1.8 %copy_bitcast_fusion = bf16[48,4096]{1,0:T(8,128)(2,1)} fusion(bf16[32,48,128]{2,1,0:T(8,128)(2,1)} %shard_map.73), kind=kLoop, calls=%fused_computation | loop fusion | bytes 786432 | tf_op jit(solution)/shard_map/reshape | solution.py:449

commit v4 on v3

--- a/solution.py
+++ b/solution.py
@@ -76,7 +76,7 @@
 
 def digits_of(n):
     bits = n.bit_length() - 1
-    return [(b, 1 << min(2, bits - b)) for b in range(0, bits, 2)]
+    return [(0, 4)] + [(b, 2) for b in range(2, bits)]
 
 
 def kernel(
@@ -90,7 +90,7 @@
     block = send.shape[2]
     n_off = off_ref.shape[1]
     digits = digits_of(n)
-    cuts = [1 + (n - 1) * i // 4 for i in (1, 2, 3)]
+    middle = n // 2
 
     kv_copy = pltpu.make_async_copy(kv_hbm, kv, kv_sem)
     kv_copy.start()
@@ -170,9 +170,8 @@
         send[c] = dot(pack, stacked).astype(BF16).reshape(n, block, PART_W)
         if c == 0:
             pl.semaphore_wait(barrier, n - 1)
-            send_rows(0, 1, n)
+        send_rows(c, 1, n)
         recv[c, me] = send[c, me]
-    send_rows(1, 1, cuts[0])
 
     my_slot = moved[me]
     pair = mask[0]
@@ -368,27 +367,26 @@
             out_ref[c * HEADS + h] = total[h * n_rows : (h + 1) * n_rows]
 
     x0 = arrive(0)
-    send_rows(1, cuts[0], cuts[1])
     kv_copy.wait()
     attend(0, 0)
     x0.step()
-    send_rows(1, cuts[1], cuts[2])
     attend(0, 1)
+    x0.step()
+    x1 = arrive(1)
     y0 = Swap(attend_visitor(0, x0.finish()), ys, yr, ys_sem, yr_sem, 0)
-    send_rows(1, cuts[2], n)
-    pack_back(0)
-    y0.step()
-    x1 = arrive(1)
     attend(1, 0)
     x1.step()
+    y0.step()
+    attend(1, 1)
+    x1.step()
+    y0.step()
+    pack_back(0)
     send_back(0, y0.finish())
-    send_answers(0, 1, cuts[1])
-    attend(1, 1)
+    send_answers(0, 1, middle)
     y1 = Swap(attend_visitor(1, x1.finish()), ys, yr, ys_sem, yr_sem, 1)
-    send_answers(0, cuts[1], cuts[2])
     pack_back(1)
     y1.step()
-    send_answers(0, cuts[2], n)
+    send_answers(0, middle, n)
     send_back(1, y1.finish())
     send_answers(1, 1, n)
     finish(0)

time: 54.6 us -> 56.1 us (1.027)
  Pallas kernels: 51.9 us -> 53.1 us
    pallas_call x1, Pallas kernels: 51.9 us -> 53.1 us  [on_device(): pl.pallas_call(functools.partial(kernel, n, cap), out_shape=jax.ShapeDtyp...]
where the time goes in v4:
time: 56.1 us; the launch traced here: 55.5 us
  Pallas kernels  53.1 us (95%)
  local copies, waits for them, and re-layouts  1.77 us (3%)
  between operations  0.66 us (1%)
    pallas_call x1, Pallas kernels, on_device(): pl.pallas_call(functools.partial(kernel, n, cap), out_shape=jax.ShapeDtyp...  53.1 us
    reshape x1, local copies, waits for them, and re-layouts, on_device(): return heads_first.transpose(1, 0, 2).reshape(n_rows, QW)  1.77 us

profile of v4, /device:TPU:0, one launch (start us, length us, event | category | flops | bytes accessed | tf_op | source)
XLA Modules:
  0.0 55.5 jit_solution(14383869777910162823)
XLA Ops:
  0.7 53.1 %shard_map.73 = bf16[32,48,128]{2,1,0:T(8,128)(2,1)} custom-call(s32[192]{0:T(256)} %lengths.1, s32[1]{0:T(128)S(6)} %copy.11.mask, s32[16]{0:T(128)} %moved.1, s32[1,48]{1,0:T(1,128)} %bitcast.8, s32[1,16]{1,0:T(1,128)} %bitcast.9, bf16[48,5120]{1,0:T(8,128)(2,1)} %draft_ref.1, bf16[36,2,128,512]{3,2,1,0:T(8,128)(2,1)} %kv_hbm.1), custom_call_target="tpu_custom_call" | custom-call | tf_op jit(solution)/shard_map/pallas_call | solution.py:411
  53.8 1.8 %copy_bitcast_fusion = bf16[48,4096]{1,0:T(8,128)(2,1)} fusion(bf16[32,48,128]{2,1,0:T(8,128)(2,1)} %shard_map.73), kind=kLoop, calls=%fused_computation | loop fusion | bytes 786432 | tf_op jit(solution)/shard_map/reshape | solution.py:447

commit v5 on v2

--- a/solution.py
+++ b/solution.py
@@ -209,21 +209,22 @@
         out_pick[m] = pick(jnp.where(out_place == m, out_from, -1), n * HEADS)
 
     class Swap:
-        def __init__(self, cur, s_ref, r_ref, s_sem, r_sem, c):
-            self.cur, self.refs, self.c = cur, (s_ref, r_ref, s_sem, r_sem), c
+        def __init__(self, parts, s_ref, r_ref, s_sem, r_sem):
+            self.cur = jnp.concatenate(parts, axis=0)
+            self.refs = (s_ref, r_ref, s_sem, r_sem)
             self.slot, self.todo = 0, list(digits)
             self.start()
 
         def start(self):
             s_ref, r_ref, s_sem, r_sem = self.refs
             shift, values = self.todo[0]
-            c, slot = self.c, self.slot
-            s_ref[c, slot] = self.cur
+            slot = self.slot
+            s_ref[slot] = self.cur
             self.copies = [
                 pltpu.make_async_remote_copy(
-                    src_ref=s_ref.at[c, slot], dst_ref=r_ref.at[c, slot + delta - 1],
-                    send_sem=s_sem.at[c, slot + delta - 1],
-                    recv_sem=r_sem.at[c, slot + delta - 1],
+                    src_ref=s_ref.at[slot], dst_ref=r_ref.at[slot + delta - 1],
+                    send_sem=s_sem.at[slot + delta - 1],
+                    recv_sem=r_sem.at[slot + delta - 1],
                     device_id={"req": flip(me, delta << shift)}, device_id_type=MESH,
                 )
                 for delta in range(1, values)
@@ -237,7 +238,7 @@
             digit = jnp.bitwise_and(jnp.right_shift(pair, shift), values - 1)
             for delta in range(1, values):
                 self.copies[delta - 1].wait()
-                self.cur = jnp.where(digit == delta, r_ref[self.c, self.slot + delta - 1], self.cur)
+                self.cur = jnp.where(digit == delta, r_ref[self.slot + delta - 1], self.cur)
             self.slot += values - 1
 
         def step(self):
@@ -248,7 +249,8 @@
         def finish(self):
             while self.todo:
                 self.step()
-            return self.cur
+            rows = self.cur.shape[0] // CHUNKS
+            return [self.cur[c * rows : (c + 1) * rows] for c in range(CHUNKS)]
 
     rows_p = 2 * DRAFT
     span = PPR * PAGE
@@ -335,9 +337,7 @@
         mine = jnp.concatenate(
             [dot(x_pick[:, : n * block], got), dot(x_pick[:, n * block :], stack)], axis=1
         ).astype(BF16)
-        x_swap = Swap(mine, xs, xr, xs_sem, xr_sem, c)
-        rows[c] = dot(unpack[...], got)
-        return x_swap
+        return mine, got
 
     def pack_back(c):
         flat_res = res[c].reshape(flat, HD).astype(BF16)
@@ -359,24 +359,27 @@
             lanes = slice((c * HEADS + h) * HD, (c * HEADS + h + 1) * HD)
             out_ref[:, lanes] = total[h * n_rows : (h + 1) * n_rows]
 
-    x0 = arrive(0)
+    mine0, got = arrive(0)
+    rows[0] = dot(unpack[...], got)
     kv_copy.wait()
     attend(0, 0)
-    x0.step()
     attend(0, 1)
-    x1 = arrive(1)
-    y0 = Swap(attend_visitor(0, x0.finish()), ys, yr, ys_sem, yr_sem, 0)
+    mine1, got = arrive(1)
+    moving = Swap([mine0, mine1], xs, xr, xs_sem, xr_sem)
+    rows[1] = dot(unpack[...], got)
     attend(1, 0)
-    x1.step()
-    y0.step()
+    moving.step()
     attend(1, 1)
+    visitors = moving.finish()
+    answers = Swap([attend_visitor(c, visitors[c]) for c in range(CHUNKS)], ys, yr, ys_sem, yr_sem)
     pack_back(0)
-    send_back(0, y0.finish())
-    y1 = Swap(attend_visitor(1, x1.finish()), ys, yr, ys_sem, yr_sem, 1)
+    answers.step()
     pack_back(1)
-    send_back(1, y1.finish())
-    finish(0)
-    finish(1)
+    final = answers.finish()
+    for c in range(CHUNKS):
+        send_back(c, final[c])
+    for c in range(CHUNKS):
+        finish(c)
     for c in range(CHUNKS):
         wait_send(send, recv, send_sem, recv_sem, c)
         wait_send(back, home, back_sem, home_sem, c)
@@ -390,8 +393,8 @@
     cap = n_rows // row_offsets.shape[0]
     block = -(-PARTS * cap // 16) * 16
     swaps = sum(values - 1 for _, values in digits_of(n))
-    x_shape = (CHUNKS, swaps, 4 * DRAFT, PART_W + HD)
-    y_shape = (CHUNKS, swaps, HEADS * DRAFT, HD)
+    x_shape = (swaps, CHUNKS * 4 * DRAFT, PART_W + HD)
+    y_shape = (swaps, CHUNKS * HEADS * DRAFT, HD)
     vmem, smem = pltpu.VMEM, pltpu.SMEM
     dma = pltpu.SemaphoreType.DMA
     return pl.pallas_call(
@@ -421,7 +424,7 @@
             vmem((cap, HEADS * n_rows, n * HEADS), BF16),
             dma,
             dma((CHUNKS, n)), dma((CHUNKS, n)), dma((CHUNKS, n)), dma((CHUNKS, n)),
-            dma((CHUNKS, swaps)), dma((CHUNKS, swaps)), dma((CHUNKS, swaps)), dma((CHUNKS, swaps)),
+            dma((swaps,)), dma((swaps,)), dma((swaps,)), dma((swaps,)),
         ],
         compiler_params=pltpu.CompilerParams(
             collective_id=0, has_side_effects=True, vmem_limit_bytes=56 * 1024 * 1024

time: 53 us -> 57 us (1.075)
  Pallas kernels: 50.3 us -> 54.4 us
    pallas_call x1, Pallas kernels: 50.3 us -> 54.4 us  [on_device(): pl.pallas_call(functools.partial(kernel, n, cap), out_shape=jax.ShapeDtyp...]
where the time goes in v5:
time: 57 us; the launch traced here: 56.9 us
  Pallas kernels  54.4 us (95%)
  local copies, waits for them, and re-layouts  1.77 us (3%)
  between operations  0.66 us (1%)
    pallas_call x1, Pallas kernels, on_device(): pl.pallas_call(functools.partial(kernel, n, cap), out_shape=jax.ShapeDtyp...  54.4 us
    unnamed x1, local copies, waits for them, and re-layouts  1.77 us

profile of v5, /device:TPU:0, one launch (start us, length us, event | category | flops | bytes accessed | tf_op | source)
XLA Modules:
  0.0 56.9 jit_solution(8673803125457312201)
XLA Ops:
  0.7 54.4 %shard_map.73 = bf16[48,4096]{1,0:T(8,128)(2,1)} custom-call(s32[192]{0:T(256)} %lengths.1, s32[1]{0:T(128)S(6)} %copy.9.mask, s32[16]{0:T(128)} %moved.1, s32[1,48]{1,0:T(1,128)} %bitcast.2, s32[1,16]{1,0:T(1,128)} %bitcast.3, bf16[48,5120]{1,0:T(8,128)(2,1)} %draft_ref.1, bf16[36,2,128,512]{3,2,1,0:T(8,128)(2,1)} %kv_hbm.1), custom_call_target="tpu_custom_call" | custom-call | tf_op jit(solution)/shard_map/pallas_call | solution.py:400
  55.1 1.8 %copy.10 = bf16[48,4096]{1,0:T(8,128)(2,1)} copy(bf16[48,4096]{1,0:T(8,128)(2,1)} %shard_map.73) | data formatting | bytes 786432

commit v6 on v2

--- a/solution.py
+++ b/solution.py
@@ -94,9 +94,15 @@
     kv_copy = pltpu.make_async_copy(kv_hbm, kv, kv_sem)
     kv_copy.start()
 
+    bits = n.bit_length() - 1
+    turn = [(1 << b) * (1 - 2 * ((me // (1 << b)) % 2)) for b in range(bits)]
+
     def peer_of(i):
-        step = (i + n // 2 - 1) % (n - 1) + 1
-        return (me + step) % n
+        place = (i + me % 2) % (n - 1) + 1
+        peer = me
+        for b in range(bits):
+            peer = peer + turn[b] * ((place // (1 << (bits - 1 - b))) % 2)
+        return peer
 
     barrier = pltpu.get_barrier_semaphore()
 
@@ -126,13 +132,14 @@
             device_id={"req": peer}, device_id_type=MESH,
         )
 
-    def send_all(s_ref, r_ref, s_sem, r_sem, c):
+    def send_all(s_ref, r_ref, s_sem, r_sem, c, lo=0, hi=n - 1):
         def body(i, carry):
             exchange(s_ref, r_ref, s_sem, r_sem, c, peer_of(i)).start()
             return carry
 
-        lax.fori_loop(0, n - 1, body, 0)
-        r_ref[c, me] = s_ref[c, me]
+        lax.fori_loop(lo, hi, body, 0)
+        if lo == 0:
+            r_ref[c, me] = s_ref[c, me]
 
     def wait_recv(s_ref, r_ref, s_sem, r_sem, c):
         def body(i, carry):
@@ -344,12 +351,14 @@
         for m in range(cap):
             partial[c, :, m * HD : (m + 1) * HD] = dot(back_pick[m], flat_res)
 
+    def send_answers(c, lo=0, hi=n - 1):
+        send_all(back, home, back_sem, home_sem, c, lo, hi)
+
     def send_back(c, answer):
         for m in range(cap):
             lanes = slice(m * HD, (m + 1) * HD)
             total = partial[c, :, lanes] + dot(y_pick[m], answer)
             back[c, :, :, lanes] = total.astype(BF16).reshape(n, HEADS, HD)
-        send_all(back, home, back_sem, home_sem, c)
 
     def finish(c):
         wait_recv(back, home, back_sem, home_sem, c)
@@ -373,8 +382,12 @@
     pack_back(0)
     send_back(0, y0.finish())
     y1 = Swap(attend_visitor(1, x1.finish()), ys, yr, ys_sem, yr_sem, 1)
+    send_answers(0, 0, n // 2)
     pack_back(1)
+    y1.step()
+    send_answers(0, n // 2)
     send_back(1, y1.finish())
+    send_answers(1)
     finish(0)
     finish(1)
     for c in range(CHUNKS):

time: 53 us -> 53.5 us (level)
  no operation moved by 1% of the time
where the time goes in v6:
time: 53.5 us; the launch traced here: 53.2 us
  Pallas kernels  50.8 us (95%)
  local copies, waits for them, and re-layouts  1.77 us (3%)
  between operations  0.66 us (1%)
    pallas_call x1, Pallas kernels, on_device(): pl.pallas_call(functools.partial(kernel, n, cap), out_shape=jax.ShapeDtyp...  50.8 us
    unnamed x1, local copies, waits for them, and re-layouts  1.77 us

profile of v6, /device:TPU:0, one launch (start us, length us, event | category | flops | bytes accessed | tf_op | source)
XLA Modules:
  0.0 53.2 jit_solution(12356344777152272179)
XLA Ops:
  0.7 50.8 %shard_map.73 = bf16[48,4096]{1,0:T(8,128)(2,1)} custom-call(s32[192]{0:T(256)} %lengths.1, s32[1]{0:T(128)S(6)} %copy.9.mask, s32[16]{0:T(128)} %moved.1, s32[1,48]{1,0:T(1,128)} %bitcast.2, s32[1,16]{1,0:T(1,128)} %bitcast.3, bf16[48,5120]{1,0:T(8,128)(2,1)} %draft_ref.1, bf16[36,2,128,512]{3,2,1,0:T(8,128)(2,1)} %kv_hbm.1), custom_call_target="tpu_custom_call" | custom-call | tf_op jit(solution)/shard_map/pallas_call | solution.py:410
  51.4 1.8 %copy.10 = bf16[48,4096]{1,0:T(8,128)(2,1)} copy(bf16[48,4096]{1,0:T(8,128)(2,1)} %shard_map.73) | data formatting | bytes 786432

commit v7 on v2

--- a/solution.py
+++ b/solution.py
@@ -82,7 +82,7 @@
 def kernel(
     n, cap, lengths, mask, moved, order_ref, off_ref, draft_ref, kv_hbm, out_ref,
     kv, send, recv, rows, res, partial, back, home, xs, xr, ys, yr,
-    unpack, x_pick, back_pick, y_pick, out_pick,
+    unpack, x_pick, back_pick, y_pick, out_pick, keys_t,
     kv_sem, send_sem, recv_sem, back_sem, home_sem, xs_sem, xr_sem, ys_sem, yr_sem,
 ):
     me = lax.axis_index("req")
@@ -281,10 +281,7 @@
             at = pr * rows_p
             slot = pr * 2
             limit = jnp.where(first, lengths[me * R_DEV + slot], lengths[me * R_DEV + slot + 1])
-            both = [
-                jnp.concatenate([cached(slot + a, which, c, g) for a in (0, 1)], axis=1)
-                for which in (0, 1)
-            ]
+            values = jnp.concatenate([cached(slot + a, 1, c, g) for a in (0, 1)], axis=1)
             tiles = []
             for h in range(GRP):
                 p, i = divmod(g * GRP + h, PART_HEADS)
@@ -296,9 +293,9 @@
             new_v = rows[c, r0 : r0 + rows_p, (KV_HERE + g) * HD : (KV_HERE + g + 1) * HD].astype(BF16)
             q2 = jnp.concatenate([jnp.where(first, q, 0.0), jnp.where(first, 0.0, q)], axis=1)
             w, new_w, total = weigh(
-                dot_t(q2.astype(BF16), both[0]), position < limit, dot_t(q.astype(BF16), new_k), new_ok
+                dot(q2.astype(BF16), keys_t[c, g, pr]), position < limit, dot_t(q.astype(BF16), new_k), new_ok
             )
-            out = dot(w, both[1])
+            out = dot(w, values)
             out = jnp.where(first, out[:, :HD], out[:, HD:]) + dot(new_w, new_v)
             res[c, g * GRP : (g + 1) * GRP, at : at + rows_p, :] = (out / total).reshape(
                 GRP, rows_p, HD
@@ -359,8 +356,14 @@
             lanes = slice((c * HEADS + h) * HD, (c * HEADS + h + 1) * HD)
             out_ref[:, lanes] = total[h * n_rows : (h + 1) * n_rows]
 
+    kv_copy.wait()
+    for c in range(CHUNKS):
+        for g in range(KV_HERE):
+            for pr in range(R_DEV // 2):
+                keys_t[c, g, pr] = jnp.concatenate(
+                    [cached(pr * 2 + a, 0, c, g) for a in (0, 1)], axis=1
+                ).T
     x0 = arrive(0)
-    kv_copy.wait()
     attend(0, 0)
     x0.step()
     attend(0, 1)
@@ -419,6 +422,7 @@
             vmem((cap, n * HEADS, HEADS * n_rows), BF16),
             vmem((cap, n * HEADS, HEADS * DRAFT), BF16),
             vmem((cap, HEADS * n_rows, n * HEADS), BF16),
+            vmem((CHUNKS, KV_HERE, R_DEV // 2, 2 * HD, PPR * PAGE), BF16),
             dma,
             dma((CHUNKS, n)), dma((CHUNKS, n)), dma((CHUNKS, n)), dma((CHUNKS, n)),
             dma((CHUNKS, swaps)), dma((CHUNKS, swaps)), dma((CHUNKS, swaps)), dma((CHUNKS, swaps)),

time: 53 us -> 52.6 us (level)
  no operation moved by 1% of the time
where the time goes in v7:
time: 52.6 us; the launch traced here: 52.5 us
  Pallas kernels  50 us (95%)
  local copies, waits for them, and re-layouts  1.77 us (3%)
  between operations  0.66 us (1%)
    pallas_call x1, Pallas kernels, on_device(): pl.pallas_call(functools.partial(kernel, n, cap), out_shape=jax.ShapeDtyp...  50 us
    unnamed x1, local copies, waits for them, and re-layouts  1.77 us

profile of v7, /device:TPU:0, one launch (start us, length us, event | category | flops | bytes accessed | tf_op | source)
XLA Modules:
  0.0 52.5 jit_solution(8713486703321291776)
XLA Ops:
  0.7 50.0 %shard_map.73 = bf16[48,4096]{1,0:T(8,128)(2,1)} custom-call(s32[192]{0:T(256)} %lengths.1, s32[1]{0:T(128)S(6)} %copy.9.mask, s32[16]{0:T(128)} %moved.1, s32[1,48]{1,0:T(1,128)} %bitcast.2, s32[1,16]{1,0:T(1,128)} %bitcast.3, bf16[48,5120]{1,0:T(8,128)(2,1)} %draft_ref.1, bf16[36,2,128,512]{3,2,1,0:T(8,128)(2,1)} %kv_hbm.1), custom_call_target="tpu_custom_call" | custom-call | tf_op jit(solution)/shard_map/pallas_call | solution.py:400
  50.7 1.8 %copy.10 = bf16[48,4096]{1,0:T(8,128)(2,1)} copy(bf16[48,4096]{1,0:T(8,128)(2,1)} %shard_map.73) | data formatting | bytes 786432

commit v8 on v7

--- a/solution.py
+++ b/solution.py
@@ -126,13 +126,14 @@
             device_id={"req": peer}, device_id_type=MESH,
         )
 
-    def send_all(s_ref, r_ref, s_sem, r_sem, c):
+    def send_all(s_ref, r_ref, s_sem, r_sem, c, lo=0, hi=n - 1):
         def body(i, carry):
             exchange(s_ref, r_ref, s_sem, r_sem, c, peer_of(i)).start()
             return carry
 
-        lax.fori_loop(0, n - 1, body, 0)
-        r_ref[c, me] = s_ref[c, me]
+        lax.fori_loop(lo, hi, body, 0)
+        if lo == 0:
+            r_ref[c, me] = s_ref[c, me]
 
     def wait_recv(s_ref, r_ref, s_sem, r_sem, c):
         def body(i, carry):
@@ -163,7 +164,7 @@
         send[c] = dot(pack, stacked).astype(BF16).reshape(n, block, PART_W)
         if c == 0:
             pl.semaphore_wait(barrier, n - 1)
-        send_all(send, recv, send_sem, recv_sem, c)
+        send_all(send, recv, send_sem, recv_sem, c, 0, n - 1 if c == 0 else n // 2)
 
     my_slot = moved[me]
     pair = mask[0]
@@ -366,15 +367,16 @@
     x0 = arrive(0)
     attend(0, 0)
     x0.step()
+    send_all(send, recv, send_sem, recv_sem, 1, n // 2)
     attend(0, 1)
+    y0 = Swap(attend_visitor(0, x0.finish()), ys, yr, ys_sem, yr_sem, 0)
+    pack_back(0)
     x1 = arrive(1)
-    y0 = Swap(attend_visitor(0, x0.finish()), ys, yr, ys_sem, yr_sem, 0)
+    y0.step()
     attend(1, 0)
     x1.step()
-    y0.step()
+    send_back(0, y0.finish())
     attend(1, 1)
-    pack_back(0)
-    send_back(0, y0.finish())
     y1 = Swap(attend_visitor(1, x1.finish()), ys, yr, ys_sem, yr_sem, 1)
     pack_back(1)
     send_back(1, y1.finish())

time: 52.6 us -> 55.5 us (1.055)
  Pallas kernels: 50 us -> 52.9 us
    pallas_call x1, Pallas kernels: 50 us -> 52.9 us  [on_device(): pl.pallas_call(functools.partial(kernel, n, cap), out_shape=jax.ShapeDtyp...]
where the time goes in v8:
time: 55.5 us; the launch traced here: 55.3 us
  Pallas kernels  52.9 us (95%)
  local copies, waits for them, and re-layouts  1.77 us (3%)
  between operations  0.66 us (1%)
    pallas_call x1, Pallas kernels, on_device(): pl.pallas_call(functools.partial(kernel, n, cap), out_shape=jax.ShapeDtyp...  52.9 us
    unnamed x1, local copies, waits for them, and re-layouts  1.77 us

profile of v8, /device:TPU:0, one launch (start us, length us, event | category | flops | bytes accessed | tf_op | source)
XLA Modules:
  0.0 55.3 jit_solution(2278980443453265867)
XLA Ops:
  0.7 52.9 %shard_map.73 = bf16[48,4096]{1,0:T(8,128)(2,1)} custom-call(s32[192]{0:T(256)} %lengths.1, s32[1]{0:T(128)S(6)} %copy.9.mask, s32[16]{0:T(128)} %moved.1, s32[1,48]{1,0:T(1,128)} %bitcast.2, s32[1,16]{1,0:T(1,128)} %bitcast.3, bf16[48,5120]{1,0:T(8,128)(2,1)} %draft_ref.1, bf16[36,2,128,512]{3,2,1,0:T(8,128)(2,1)} %kv_hbm.1), custom_call_target="tpu_custom_call" | custom-call | tf_op jit(solution)/shard_map/pallas_call | solution.py:402
  53.6 1.8 %copy.10 = bf16[48,4096]{1,0:T(8,128)(2,1)} copy(bf16[48,4096]{1,0:T(8,128)(2,1)} %shard_map.73) | data formatting | bytes 786432
